TPU v7x, 256 devices: a whole 4x4x8 slice. The times are simulated.
256 devices in a mesh: tm: 8 (over y, x_hi), space: 32 (over z, x_lo, core).
Axes of the slice: x: 4 (x_hi: 2, x_lo: 2; x = x_hi * 2 + x_lo), y: 4, z: 8, core: 2. Of those that a mesh axis runs over, the one named last changes fastest.
Arguments:
- starts: float32 [8, 3, 256, 32, 128], P('tm', None, 'space'), may hold values from -6 to 6
- source: float32 [8, 3, 256, 32, 128], P('tm', None, 'space'), may hold values from -6 to 6
- mass_term: float32 [256, 32, 128], P('space'), may hold values from 0.5 to 4
- curve_entry: int32 [256, 32, 128], P('space'), may hold values from 0 to 63
- curve_table: float32 [2, 64], replicated, may hold values from 0.3 to 3
Outputs:
- next_starts: float32 [8, 3, 256, 32, 128], P('tm', None, 'space')
All inputs are finite; a program needn't handle non-finite values.
Results may differ from a plain program's by a relative error of at most 0.00002.
Values sent between devices are 32-bit elements; how exact they have to be, the bound alone decides.
A program may use at most 64 MiB of HBM per device.

v0:
```python
import jax
import jax.numpy as jnp
from jax import lax
from jax.sharding import PartitionSpec as P

STEPS = 2
UPDATES = 2
SWEEPS = 4
C_SWEEPS = 2


relaxation = 0.45


def shifted_2(value, axis, steps):
    count = lax.axis_size(axis)
    first, last = (max(0, -steps), min(count, count - steps))
    return lax.ppermute(value, axis, [(source, source + steps) for source in range(first, last)])


def from_behind(block, axis, distance):
    devices = range(lax.axis_size(axis))
    route = [((i - distance) % len(devices), i) for i in devices]
    return lax.ppermute(block, axis, route)


def curl_forward(potential, shifted):
    along_z = shifted - potential
    along_y = jnp.roll(potential, -1, -2) - potential
    along_x = jnp.roll(potential, -1, -1) - potential
    return jnp.stack([along_y[2] - along_z[1], along_z[0] - along_x[2], along_x[1] - along_y[0]])


def curl_adjoint(intensity, lower_plane):
    before = jnp.concatenate([lower_plane[:, None], intensity[:, :-1]], axis=1)
    along_z = before - intensity
    along_y = jnp.roll(intensity, 1, -2) - intensity
    along_x = jnp.roll(intensity, 1, -1) - intensity
    return jnp.stack([along_z[1] - along_y[2], along_x[2] - along_z[0], along_y[0] - along_x[1]])


def reluctance(induction, base_value, saturation):
    squared = (
        induction[0] * induction[0] + induction[1] * induction[1] + induction[2] * induction[2]
    )
    return base_value * (1.0 + saturation * squared / (1.0 + squared))


def diagonal(reluct_cell, lower_plane, mass_term):
    before_z = jnp.concatenate([lower_plane[None], reluct_cell[:-1]], axis=0)
    before_y = jnp.roll(reluct_cell, 1, -2)
    before_x = jnp.roll(reluct_cell, 1, -1)
    doubled = 2.0 * reluct_cell
    return jnp.stack(
        [
            mass_term + doubled + before_z + before_y,
            mass_term + doubled + before_z + before_x,
            mass_term + doubled + before_y + before_x,
        ]
    )


def upper_planes(potential):
    upper_plane = shifted_2(potential[:, 0], "space", -1)
    return jnp.concatenate([potential[:, 1:], upper_plane[:, None]], axis=1)


def curve_lookup(curve_entry, curve_table):

    def accumulate(entry_index, totals):
        matched = curve_entry == entry_index
        return (
            totals[0] + jnp.where(matched, curve_table[0, entry_index], 0.0),
            totals[1] + jnp.where(matched, curve_table[1, entry_index], 0.0),
        )

    zeros_cells = jnp.zeros(curve_entry.shape, jnp.float32)
    return lax.fori_loop(0, curve_table.shape[1], accumulate, (zeros_cells, zeros_cells))


def frozen_update(initial, right_side, mass_term, sweeps, material):
    base_value, saturation, base_wide, saturation_wide, material_deep = material
    potential = initial
    induction = curl_forward(initial, upper_planes(initial))
    reluct_cell = reluctance(induction, base_value, saturation)
    lower_plane = shifted_2(reluct_cell[-1], "space", 1)
    diagonal_terms = diagonal(reluct_cell, lower_plane, mass_term)
    for sweep_index in range(sweeps):
        if sweep_index > 0:
            induction = curl_forward(potential, upper_planes(potential))
        intensity = reluct_cell[None] * induction
        intensity_below = shifted_2(intensity[:, -1], "space", 1)
        operator_image = mass_term * potential + curl_adjoint(intensity, intensity_below)
        potential = potential + relaxation * (right_side - operator_image) / diagonal_terms
    return potential


def body(starts, source, mass_term, curve_entry, curve_table):
    base_value, saturation = curve_lookup(curve_entry, curve_table)
    material_deep = base_value[None]
    material = (base_value, saturation, base_value, saturation, material_deep)
    initial = starts[0]
    current = source[0]
    potential = initial
    for step_index in range(STEPS):
        right_side = mass_term * potential + current
        for update_index in range(UPDATES):
            potential = frozen_update(potential, right_side, mass_term, SWEEPS, material)
    coarse_mass = mass_term / STEPS
    old_coarse = frozen_update(
        initial, coarse_mass * initial + current, coarse_mass, C_SWEEPS, material
    )
    correction = potential - old_coarse
    position = lax.axis_index("tm")
    groups = lax.axis_size("tm")
    payload = jnp.where(position == groups - 1, potential, correction)
    received = from_behind(payload, "tm", 1)

    def link_passed(link_index, carried):
        coarse_next = frozen_update(
            carried, coarse_mass * carried + current, coarse_mass, C_SWEEPS, material
        )
        arrived = shifted_2(coarse_next, "tm", 1)
        return jnp.where(position == link_index + 1, arrived + received, carried)

    result = lax.fori_loop(0, groups - 1, link_passed, received)
    return result[None]


def solution(mesh):
    return jax.shard_map(
        body,
        mesh=mesh,
        in_specs=(
            P("tm", None, "space", None, None),
            P("tm", None, "space", None, None),
            P("space", None, None),
            P("space", None, None),
            P(),
        ),
        out_specs=P("tm", None, "space", None, None),
        check_vma=False,
    )
```

profile of v0, /device:TPU:106, one launch (start us, length us, event | category | flops | bytes accessed | tf_op | source)
XLA Modules:
  0.0 724.9 jit_solution(6672302139951166266)
XLA Ops:
  3.4 180.2 %while.30 = (s32[]{:T(128)}, f32[8,32,128]{2,1,0:T(8,128)S(1)}, f32[8,32,128]{2,1,0:T(8,128)S(1)}, s32[8,32,128]{2,1,0:T(8,128)}, f32[2,64]{1,0:T(2,128)S(1)}, /*index=5*/s32[]{:T(128)}, s32[]{:T(128)}) while((s32[]{:T(128)}, f32[8,32,128]{2,1,0:T(8,128)S(1)}, f32[8,32,128]{2,1,0:T(8,128)S(1)}, s32[8,32,128]{2,1,0:T(8,128)}, ...), condition=%wide.region_1.2_spmd.clone, body=%wide.region_0.1_spmd.clone.sunk | while | flops 229379 | bytes 721024 | solution.py:78
  184.3 2.4 collective-permute-start.8
  187.1 5.1 collective-permute-start.7
  197.1 2.9 collective-permute-start.9
  202.2 5.7 collective-permute-start.10
  213.4 6.7 collective-permute-start.12
  225.5 6.7 collective-permute-start.14
  237.6 6.7 collective-permute-start.17
  246.8 3.3 collective-permute-done.16
  254.7 4.1 collective-permute-start.19
  264.7 6.2 collective-permute-start.21
  276.3 6.9 collective-permute-start.23
  288.4 6.7 collective-permute-start.26
  297.6 3.3 collective-permute-done.25
  305.5 4.1 collective-permute-start.28
  315.5 6.2 collective-permute-start.30
  327.1 6.7 collective-permute-start.32
  339.2 6.7 collective-permute-start.35
  348.4 3.3 collective-permute-done.34
  356.3 4.1 collective-permute-start.37
  366.3 6.2 collective-permute-start.39
  375.4 3.6 collective-permute-start.40
  381.1 4.3 collective-permute-start.41
  388.3 2.5 collective-permute-start.44
  391.3 10.3 %collective-permute-done.44 = f32[3,8,32,128]{3,2,1,0:T(8,128)S(1)} collective-permute-done((f32[3,8,32,128]{3,2,1,0:T(8,128)S(1)}, f32[3,8,32,128]{3,2,1,0:T(8,128)S(1)}, u32[]{:S(2)}, u32[]{:S(2)}) %collective-permute-start.44) | collective-permute-done | bytes 393248 | tf_op jit(solution)/shard_map/ppermute | solution.py:24
  402.0 322.1 %while.29 = (s32[]{:T(128)}, f32[3,8,32,128]{3,1,2,0:T(8,128)S(1)}, s32[]{:T(128)}, f32[8,32,128]{2,0,1:T(8,128)S(1)}, f32[3,8,32,128]{3,1,2,0:T(8,128)S(1)}, /*...) while((s32[]{:T(128)}, f32[3,8,32,128]{3,1,2,0:T(8,128)S(1)}, ...), condition=%wide.region_3.4_spmd, body=%wide.region_2.3_spmd.sunk | while | flops 7471107 | bytes 37228884 | solution.py:126
  406.1 4.7 collective-permute-start.1
  414.7 2.5 collective-permute-done.2
  420.0 2.6 collective-permute-done.3
  422.9 7.4 %collective-permute-start.4 = (f32[3,32,128]{2,1,0:T(8,128)S(1)}, f32[3,32,128]{2,1,0:T(8,128)S(1)}, u32[]{:S(2)}, u32[]{:S(2)}) collective-permute-start(f32[3,32,128]{2,1,0:T(8,128)S(1)} %bitcast.528), channel_id=1, source_target_pairs={{0,1},{1,2},{2,3},{3,4},{4,5},{5,6},{6,7},{7,8},{8,9},{9,10},{10,1... | collective-permute-start | bytes 147464 | tf_op jit(solution)/shard_map/while/body/eval_jaxpr/ppermute | solution.py:18
  431.6 3.4 collective-permute-start.5
  435.1 12.2 %collective-permute-done.5 = f32[3,8,32,128]{3,1,2,0:T(8,128)S(1)} collective-permute-done((f32[3,8,32,128]{3,1,2,0:T(8,128)S(1)}, f32[3,8,32,128]{3,1,2,0:T(8,128)S(1)}, u32[]{:S(2)}, u32[]{:S(2)}) %collective-permute-start.5) | collective-permute-done | bytes 393248 | tf_op jit(solution)/shard_map/while/body/eval_jaxpr/ppermute | solution.py:18
  451.6 5.3 collective-permute-start.1
  460.8 2.5 collective-permute-done.2
  466.1 2.6 collective-permute-done.3
  469.0 7.4 %collective-permute-start.4 = (f32[3,32,128]{2,1,0:T(8,128)S(1)}, f32[3,32,128]{2,1,0:T(8,128)S(1)}, u32[]{:S(2)}, u32[]{:S(2)}) collective-permute-start(f32[3,32,128]{2,1,0:T(8,128)S(1)} %bitcast.528), channel_id=1, source_target_pairs={{0,1},{1,2},{2,3},{3,4},{4,5},{5,6},{6,7},{7,8},{8,9},{9,10},{10,1... | collective-permute-start | bytes 147464 | tf_op jit(solution)/shard_map/while/body/eval_jaxpr/ppermute | solution.py:18
  477.7 2.5 collective-permute-start.5
  480.3 13.1 %collective-permute-done.5 = f32[3,8,32,128]{3,1,2,0:T(8,128)S(1)} collective-permute-done((f32[3,8,32,128]{3,1,2,0:T(8,128)S(1)}, f32[3,8,32,128]{3,1,2,0:T(8,128)S(1)}, u32[]{:S(2)}, u32[]{:S(2)}) %collective-permute-start.5) | collective-permute-done | bytes 393248 | tf_op jit(solution)/shard_map/while/body/eval_jaxpr/ppermute | solution.py:18
  497.7 5.3 collective-permute-start.1
  506.9 2.5 collective-permute-done.2
  512.2 2.6 collective-permute-done.3
  515.1 7.4 %collective-permute-start.4 = (f32[3,32,128]{2,1,0:T(8,128)S(1)}, f32[3,32,128]{2,1,0:T(8,128)S(1)}, u32[]{:S(2)}, u32[]{:S(2)}) collective-permute-start(f32[3,32,128]{2,1,0:T(8,128)S(1)} %bitcast.528), channel_id=1, source_target_pairs={{0,1},{1,2},{2,3},{3,4},{4,5},{5,6},{6,7},{7,8},{8,9},{9,10},{10,1... | collective-permute-start | bytes 147464 | tf_op jit(solution)/shard_map/while/body/eval_jaxpr/ppermute | solution.py:18
  525.8 13.7 %collective-permute-done.5 = f32[3,8,32,128]{3,1,2,0:T(8,128)S(1)} collective-permute-done((f32[3,8,32,128]{3,1,2,0:T(8,128)S(1)}, f32[3,8,32,128]{3,1,2,0:T(8,128)S(1)}, u32[]{:S(2)}, u32[]{:S(2)}) %collective-permute-start.5) | collective-permute-done | bytes 393248 | tf_op jit(solution)/shard_map/while/body/eval_jaxpr/ppermute | solution.py:18
  543.8 5.3 collective-permute-start.1
  550.1 2.3 collective-permute-start.2
  553.0 2.5 collective-permute-done.2
  558.3 2.6 collective-permute-done.3
  561.2 7.4 %collective-permute-start.4 = (f32[3,32,128]{2,1,0:T(8,128)S(1)}, f32[3,32,128]{2,1,0:T(8,128)S(1)}, u32[]{:S(2)}, u32[]{:S(2)}) collective-permute-start(f32[3,32,128]{2,1,0:T(8,128)S(1)} %bitcast.528), channel_id=1, source_target_pairs={{0,1},{1,2},{2,3},{3,4},{4,5},{5,6},{6,7},{7,8},{8,9},{9,10},{10,1... | collective-permute-start | bytes 147464 | tf_op jit(solution)/shard_map/while/body/eval_jaxpr/ppermute | solution.py:18
  571.9 13.7 %collective-permute-done.5 = f32[3,8,32,128]{3,1,2,0:T(8,128)S(1)} collective-permute-done((f32[3,8,32,128]{3,1,2,0:T(8,128)S(1)}, f32[3,8,32,128]{3,1,2,0:T(8,128)S(1)}, u32[]{:S(2)}, u32[]{:S(2)}) %collective-permute-start.5) | collective-permute-done | bytes 393248 | tf_op jit(solution)/shard_map/while/body/eval_jaxpr/ppermute | solution.py:18
  589.9 5.3 collective-permute-start.1
  599.1 2.5 collective-permute-done.2
  604.4 2.6 collective-permute-done.3
  607.3 7.4 %collective-permute-start.4 = (f32[3,32,128]{2,1,0:T(8,128)S(1)}, f32[3,32,128]{2,1,0:T(8,128)S(1)}, u32[]{:S(2)}, u32[]{:S(2)}) collective-permute-start(f32[3,32,128]{2,1,0:T(8,128)S(1)} %bitcast.528), channel_id=1, source_target_pairs={{0,1},{1,2},{2,3},{3,4},{4,5},{5,6},{6,7},{7,8},{8,9},{9,10},{10,1... | collective-permute-start | bytes 147464 | tf_op jit(solution)/shard_map/while/body/eval_jaxpr/ppermute | solution.py:18
  618.0 13.7 %collective-permute-done.5 = f32[3,8,32,128]{3,1,2,0:T(8,128)S(1)} collective-permute-done((f32[3,8,32,128]{3,1,2,0:T(8,128)S(1)}, f32[3,8,32,128]{3,1,2,0:T(8,128)S(1)}, u32[]{:S(2)}, u32[]{:S(2)}) %collective-permute-start.5) | collective-permute-done | bytes 393248 | tf_op jit(solution)/shard_map/while/body/eval_jaxpr/ppermute | solution.py:18
  636.0 5.3 collective-permute-start.1
  645.2 2.5 collective-permute-done.2
  650.5 2.6 collective-permute-done.3
  653.4 7.4 %collective-permute-start.4 = (f32[3,32,128]{2,1,0:T(8,128)S(1)}, f32[3,32,128]{2,1,0:T(8,128)S(1)}, u32[]{:S(2)}, u32[]{:S(2)}) collective-permute-start(f32[3,32,128]{2,1,0:T(8,128)S(1)} %bitcast.528), channel_id=1, source_target_pairs={{0,1},{1,2},{2,3},{3,4},{4,5},{5,6},{6,7},{7,8},{8,9},{9,10},{10,1... | collective-permute-start | bytes 147464 | tf_op jit(solution)/shard_map/while/body/eval_jaxpr/ppermute | solution.py:18
  664.1 13.7 %collective-permute-done.5 = f32[3,8,32,128]{3,1,2,0:T(8,128)S(1)} collective-permute-done((f32[3,8,32,128]{3,1,2,0:T(8,128)S(1)}, f32[3,8,32,128]{3,1,2,0:T(8,128)S(1)}, u32[]{:S(2)}, u32[]{:S(2)}) %collective-permute-start.5) | collective-permute-done | bytes 393248 | tf_op jit(solution)/shard_map/while/body/eval_jaxpr/ppermute | solution.py:18
  682.1 5.3 collective-permute-start.1
  691.3 2.5 collective-permute-done.2
  696.6 2.6 collective-permute-done.3
  699.5 7.4 %collective-permute-start.4 = (f32[3,32,128]{2,1,0:T(8,128)S(1)}, f32[3,32,128]{2,1,0:T(8,128)S(1)}, u32[]{:S(2)}, u32[]{:S(2)}) collective-permute-start(f32[3,32,128]{2,1,0:T(8,128)S(1)} %bitcast.528), channel_id=1, source_target_pairs={{0,1},{1,2},{2,3},{3,4},{4,5},{5,6},{6,7},{7,8},{8,9},{9,10},{10,1... | collective-permute-start | bytes 147464 | tf_op jit(solution)/shard_map/while/body/eval_jaxpr/ppermute | solution.py:18
  710.2 13.7 %collective-permute-done.5 = f32[3,8,32,128]{3,1,2,0:T(8,128)S(1)} collective-permute-done((f32[3,8,32,128]{3,1,2,0:T(8,128)S(1)}, f32[3,8,32,128]{3,1,2,0:T(8,128)S(1)}, u32[]{:S(2)}, u32[]{:S(2)}) %collective-permute-start.5) | collective-permute-done | bytes 393248 | tf_op jit(solution)/shard_map/while/body/eval_jaxpr/ppermute | solution.py:18
  (881 shorter events, 367.4 us)
Async XLA Ops:
  0.8 183.1 %collective-permute-start.6 = (f32[3,32,128]{2,1,0:T(8,128)S(1)}, f32[3,32,128]{2,1,0:T(8,128)S(1)}, u32[]{:S(2)}, u32[]{:S(2)}) collective-permute-start(f32[3,32,128]{2,1,0:T(8,128)S(1)} %slice_bitcast_fusion.38), channel_id=1, source_target_pairs={{1,0},{2,1},{3,2},{4,3},{5,4},{6,5},{7,6},{8,7},{9,8},{10,9},{11,1... | collective-permute-start | bytes 147464 | tf_op jit(solution)/shard_map/ppermute | solution.py:18
  184.3 7.9 %collective-permute-start.8 = (f32[32,128]{1,0:T(8,128)S(1)}, f32[32,128]{1,0:T(8,128)S(1)}, u32[]{:S(2)}, u32[]{:S(2)}) collective-permute-start(f32[32,128]{1,0:T(8,128)S(1)} %slice_bitcast_fusion.42), channel_id=1, source_target_pairs={{0,1},{1,2},{2,3},{3,4},{4,5},{5,6},{6,7},{7,8},{8,9},{9,10},{10,1... | collective-permute-start | bytes 49160 | tf_op jit(solution)/shard_map/ppermute | solution.py:18
  187.1 6.0 collective-permute-start.7
  194.6 5.4 collective-permute-start.42
  197.1 4.6 collective-permute-start.9
  202.2 6.6 collective-permute-start.10
  209.3 3.7 collective-permute-start.11
  213.4 7.5 %collective-permute-start.12 = (f32[3,32,128]{2,1,0:T(8,128)S(1)}, f32[3,32,128]{2,1,0:T(8,128)S(1)}, u32[]{:S(2)}, u32[]{:S(2)}) collective-permute-start(f32[3,32,128]{2,1,0:T(8,128)S(1)} %slice_bitcast_fusion.33), channel_id=1, source_target_pairs={{0,1},{1,2},{2,3},{3,4},{4,5},{5,6},{6,7},{7,8},{8,9},{9,10},{10,1... | collective-permute-start | bytes 147464 | tf_op jit(solution)/shard_map/ppermute | solution.py:18
  221.5 3.7 collective-permute-start.13
  225.5 7.5 %collective-permute-start.14 = (f32[3,32,128]{2,1,0:T(8,128)S(1)}, f32[3,32,128]{2,1,0:T(8,128)S(1)}, u32[]{:S(2)}, u32[]{:S(2)}) collective-permute-start(f32[3,32,128]{2,1,0:T(8,128)S(1)} %slice_bitcast_fusion.31), channel_id=1, source_target_pairs={{0,1},{1,2},{2,3},{3,4},{4,5},{5,6},{6,7},{7,8},{8,9},{9,10},{10,1... | collective-permute-start | bytes 147464 | tf_op jit(solution)/shard_map/ppermute | solution.py:18
  233.6 3.7 collective-permute-start.15
  237.6 9.0 %collective-permute-start.17 = (f32[32,128]{1,0:T(8,128)S(1)}, f32[32,128]{1,0:T(8,128)S(1)}, u32[]{:S(2)}, u32[]{:S(2)}) collective-permute-start(f32[32,128]{1,0:T(8,128)S(1)} %slice_bitcast_fusion.41), channel_id=1, source_target_pairs={{0,1},{1,2},{2,3},{3,4},{4,5},{5,6},{6,7},{7,8},{8,9},{9,10},{10,1... | collective-permute-start | bytes 49160 | tf_op jit(solution)/shard_map/ppermute | solution.py:18
  244.7 5.4 collective-permute-start.16
  254.7 5.4 collective-permute-start.19
  264.7 7.0 collective-permute-start.21
  276.3 7.5 %collective-permute-start.23 = (f32[3,32,128]{2,1,0:T(8,128)S(1)}, f32[3,32,128]{2,1,0:T(8,128)S(1)}, u32[]{:S(2)}, u32[]{:S(2)}) collective-permute-start(f32[3,32,128]{2,1,0:T(8,128)S(1)} %slice_bitcast_fusion.23), channel_id=1, source_target_pairs={{0,1},{1,2},{2,3},{3,4},{4,5},{5,6},{6,7},{7,8},{8,9},{9,10},{10,1... | collective-permute-start | bytes 147464 | tf_op jit(solution)/shard_map/ppermute | solution.py:18
  288.4 9.0 %collective-permute-start.26 = (f32[32,128]{1,0:T(8,128)S(1)}, f32[32,128]{1,0:T(8,128)S(1)}, u32[]{:S(2)}, u32[]{:S(2)}) collective-permute-start(f32[32,128]{1,0:T(8,128)S(1)} %slice_bitcast_fusion.40), channel_id=1, source_target_pairs={{0,1},{1,2},{2,3},{3,4},{4,5},{5,6},{6,7},{7,8},{8,9},{9,10},{10,1... | collective-permute-start | bytes 49160 | tf_op jit(solution)/shard_map/ppermute | solution.py:18
  295.5 5.4 collective-permute-start.25
  305.5 5.4 collective-permute-start.28
  315.5 7.0 collective-permute-start.30
  327.1 7.5 %collective-permute-start.32 = (f32[3,32,128]{2,1,0:T(8,128)S(1)}, f32[3,32,128]{2,1,0:T(8,128)S(1)}, u32[]{:S(2)}, u32[]{:S(2)}) collective-permute-start(f32[3,32,128]{2,1,0:T(8,128)S(1)} %slice_bitcast_fusion.15), channel_id=1, source_target_pairs={{0,1},{1,2},{2,3},{3,4},{4,5},{5,6},{6,7},{7,8},{8,9},{9,10},{10,1... | collective-permute-start | bytes 147464 | tf_op jit(solution)/shard_map/ppermute | solution.py:18
  339.2 9.0 %collective-permute-start.35 = (f32[32,128]{1,0:T(8,128)S(1)}, f32[32,128]{1,0:T(8,128)S(1)}, u32[]{:S(2)}, u32[]{:S(2)}) collective-permute-start(f32[32,128]{1,0:T(8,128)S(1)} %slice_bitcast_fusion.39), channel_id=1, source_target_pairs={{0,1},{1,2},{2,3},{3,4},{4,5},{5,6},{6,7},{7,8},{8,9},{9,10},{10,1... | collective-permute-start | bytes 49160 | tf_op jit(solution)/shard_map/ppermute | solution.py:18
  346.3 5.4 collective-permute-start.34
  356.3 5.4 collective-permute-start.37
  366.3 8.6 %collective-permute-start.39 = (f32[3,32,128]{2,1,0:T(8,128)S(1)}, f32[3,32,128]{2,1,0:T(8,128)S(1)}, u32[]{:S(2)}, u32[]{:S(2)}) collective-permute-start(f32[3,32,128]{2,1,0:T(8,128)S(1)} %slice_bitcast_fusion.9), channel_id=1, source_target_pairs={{0,1},{1,2},{2,3},{3,4},{4,5},{5,6},{6,7},{7,8},{8,9},{9,10},{10,1... | collective-permute-start | bytes 147464 | tf_op jit(solution)/shard_map/ppermute | solution.py:18
  372.7 6.4 collective-permute-start.43
  375.4 5.4 collective-permute-start.40
  381.1 5.4 collective-permute-start.41
  388.3 13.3 %collective-permute-start.44 = (f32[3,8,32,128]{3,2,1,0:T(8,128)S(1)}, f32[3,8,32,128]{3,2,1,0:T(8,128)S(1)}, u32[]{:S(2)}, u32[]{:S(2)}) collective-permute-start(f32[3,8,32,128]{3,2,1,0:T(8,128)S(1)} %subtract_select_fusion), channel_id=1, source_target_pairs={{224,0},{0,32},{32,64},{64,96},{96,128},{128,160},{160,192},{192,2... | collective-permute-start | bytes 1179656 | tf_op jit(solution)/shard_map/ppermute | solution.py:24
  406.1 5.6 collective-permute-start.1
  411.9 5.4 collective-permute-start.2
  417.8 4.7 collective-permute-start.3
  422.9 8.3 %collective-permute-start.4 = (f32[3,32,128]{2,1,0:T(8,128)S(1)}, f32[3,32,128]{2,1,0:T(8,128)S(1)}, u32[]{:S(2)}, u32[]{:S(2)}) collective-permute-start(f32[3,32,128]{2,1,0:T(8,128)S(1)} %bitcast.528), channel_id=1, source_target_pairs={{0,1},{1,2},{2,3},{3,4},{4,5},{5,6},{6,7},{7,8},{8,9},{9,10},{10,1... | collective-permute-start | bytes 147464 | tf_op jit(solution)/shard_map/while/body/eval_jaxpr/ppermute | solution.py:18
  431.6 15.7 %collective-permute-start.5 = (f32[3,8,32,128]{3,1,2,0:T(8,128)S(1)}, f32[3,8,32,128]{3,1,2,0:T(8,128)S(1)}, u32[]{:S(2)}, u32[]{:S(2)}) collective-permute-start(f32[3,8,32,128]{3,1,2,0:T(8,128)S(1)} %fusion.102), channel_id=1, source_target_pairs={{0,32},{32,64},{64,96},{96,128},{128,160},{160,192},{192,224},{1,3... | collective-permute-start | bytes 1179656 | tf_op jit(solution)/shard_map/while/body/eval_jaxpr/ppermute | solution.py:18
  451.6 6.1 collective-permute-start.1
  458.0 5.4 collective-permute-start.2
  463.9 4.7 collective-permute-start.3
  469.0 8.3 %collective-permute-start.4 = (f32[3,32,128]{2,1,0:T(8,128)S(1)}, f32[3,32,128]{2,1,0:T(8,128)S(1)}, u32[]{:S(2)}, u32[]{:S(2)}) collective-permute-start(f32[3,32,128]{2,1,0:T(8,128)S(1)} %bitcast.528), channel_id=1, source_target_pairs={{0,1},{1,2},{2,3},{3,4},{4,5},{5,6},{6,7},{7,8},{8,9},{9,10},{10,1... | collective-permute-start | bytes 147464 | tf_op jit(solution)/shard_map/while/body/eval_jaxpr/ppermute | solution.py:18
  477.7 15.7 %collective-permute-start.5 = (f32[3,8,32,128]{3,1,2,0:T(8,128)S(1)}, f32[3,8,32,128]{3,1,2,0:T(8,128)S(1)}, u32[]{:S(2)}, u32[]{:S(2)}) collective-permute-start(f32[3,8,32,128]{3,1,2,0:T(8,128)S(1)} %fusion.102), channel_id=1, source_target_pairs={{0,32},{32,64},{64,96},{96,128},{128,160},{160,192},{192,224},{1,3... | collective-permute-start | bytes 1179656 | tf_op jit(solution)/shard_map/while/body/eval_jaxpr/ppermute | solution.py:18
  497.7 6.1 collective-permute-start.1
  504.0 5.4 collective-permute-start.2
  510.0 4.7 collective-permute-start.3
  515.1 8.3 %collective-permute-start.4 = (f32[3,32,128]{2,1,0:T(8,128)S(1)}, f32[3,32,128]{2,1,0:T(8,128)S(1)}, u32[]{:S(2)}, u32[]{:S(2)}) collective-permute-start(f32[3,32,128]{2,1,0:T(8,128)S(1)} %bitcast.528), channel_id=1, source_target_pairs={{0,1},{1,2},{2,3},{3,4},{4,5},{5,6},{6,7},{7,8},{8,9},{9,10},{10,1... | collective-permute-start | bytes 147464 | tf_op jit(solution)/shard_map/while/body/eval_jaxpr/ppermute | solution.py:18
  523.8 15.7 %collective-permute-start.5 = (f32[3,8,32,128]{3,1,2,0:T(8,128)S(1)}, f32[3,8,32,128]{3,1,2,0:T(8,128)S(1)}, u32[]{:S(2)}, u32[]{:S(2)}) collective-permute-start(f32[3,8,32,128]{3,1,2,0:T(8,128)S(1)} %fusion.102), channel_id=1, source_target_pairs={{0,32},{32,64},{64,96},{96,128},{128,160},{160,192},{192,224},{1,3... | collective-permute-start | bytes 1179656 | tf_op jit(solution)/shard_map/while/body/eval_jaxpr/ppermute | solution.py:18
  543.8 6.1 collective-permute-start.1
  550.1 5.4 collective-permute-start.2
  556.1 4.7 collective-permute-start.3
  561.2 8.3 %collective-permute-start.4 = (f32[3,32,128]{2,1,0:T(8,128)S(1)}, f32[3,32,128]{2,1,0:T(8,128)S(1)}, u32[]{:S(2)}, u32[]{:S(2)}) collective-permute-start(f32[3,32,128]{2,1,0:T(8,128)S(1)} %bitcast.528), channel_id=1, source_target_pairs={{0,1},{1,2},{2,3},{3,4},{4,5},{5,6},{6,7},{7,8},{8,9},{9,10},{10,1... | collective-permute-start | bytes 147464 | tf_op jit(solution)/shard_map/while/body/eval_jaxpr/ppermute | solution.py:18
  569.9 15.7 %collective-permute-start.5 = (f32[3,8,32,128]{3,1,2,0:T(8,128)S(1)}, f32[3,8,32,128]{3,1,2,0:T(8,128)S(1)}, u32[]{:S(2)}, u32[]{:S(2)}) collective-permute-start(f32[3,8,32,128]{3,1,2,0:T(8,128)S(1)} %fusion.102), channel_id=1, source_target_pairs={{0,32},{32,64},{64,96},{96,128},{128,160},{160,192},{192,224},{1,3... | collective-permute-start | bytes 1179656 | tf_op jit(solution)/shard_map/while/body/eval_jaxpr/ppermute | solution.py:18
  589.9 6.1 collective-permute-start.1
  596.2 5.4 collective-permute-start.2
  602.2 4.7 collective-permute-start.3
  607.3 8.3 %collective-permute-start.4 = (f32[3,32,128]{2,1,0:T(8,128)S(1)}, f32[3,32,128]{2,1,0:T(8,128)S(1)}, u32[]{:S(2)}, u32[]{:S(2)}) collective-permute-start(f32[3,32,128]{2,1,0:T(8,128)S(1)} %bitcast.528), channel_id=1, source_target_pairs={{0,1},{1,2},{2,3},{3,4},{4,5},{5,6},{6,7},{7,8},{8,9},{9,10},{10,1... | collective-permute-start | bytes 147464 | tf_op jit(solution)/shard_map/while/body/eval_jaxpr/ppermute | solution.py:18
  616.0 15.7 %collective-permute-start.5 = (f32[3,8,32,128]{3,1,2,0:T(8,128)S(1)}, f32[3,8,32,128]{3,1,2,0:T(8,128)S(1)}, u32[]{:S(2)}, u32[]{:S(2)}) collective-permute-start(f32[3,8,32,128]{3,1,2,0:T(8,128)S(1)} %fusion.102), channel_id=1, source_target_pairs={{0,32},{32,64},{64,96},{96,128},{128,160},{160,192},{192,224},{1,3... | collective-permute-start | bytes 1179656 | tf_op jit(solution)/shard_map/while/body/eval_jaxpr/ppermute | solution.py:18
  636.0 6.1 collective-permute-start.1
  642.3 5.4 collective-permute-start.2
  648.3 4.7 collective-permute-start.3
  653.4 8.3 %collective-permute-start.4 = (f32[3,32,128]{2,1,0:T(8,128)S(1)}, f32[3,32,128]{2,1,0:T(8,128)S(1)}, u32[]{:S(2)}, u32[]{:S(2)}) collective-permute-start(f32[3,32,128]{2,1,0:T(8,128)S(1)} %bitcast.528), channel_id=1, source_target_pairs={{0,1},{1,2},{2,3},{3,4},{4,5},{5,6},{6,7},{7,8},{8,9},{9,10},{10,1... | collective-permute-start | bytes 147464 | tf_op jit(solution)/shard_map/while/body/eval_jaxpr/ppermute | solution.py:18
  662.1 15.7 %collective-permute-start.5 = (f32[3,8,32,128]{3,1,2,0:T(8,128)S(1)}, f32[3,8,32,128]{3,1,2,0:T(8,128)S(1)}, u32[]{:S(2)}, u32[]{:S(2)}) collective-permute-start(f32[3,8,32,128]{3,1,2,0:T(8,128)S(1)} %fusion.102), channel_id=1, source_target_pairs={{0,32},{32,64},{64,96},{96,128},{128,160},{160,192},{192,224},{1,3... | collective-permute-start | bytes 1179656 | tf_op jit(solution)/shard_map/while/body/eval_jaxpr/ppermute | solution.py:18
  682.1 6.1 collective-permute-start.1
  688.4 5.4 collective-permute-start.2
  694.4 4.7 collective-permute-start.3
  699.5 8.3 %collective-permute-start.4 = (f32[3,32,128]{2,1,0:T(8,128)S(1)}, f32[3,32,128]{2,1,0:T(8,128)S(1)}, u32[]{:S(2)}, u32[]{:S(2)}) collective-permute-start(f32[3,32,128]{2,1,0:T(8,128)S(1)} %bitcast.528), channel_id=1, source_target_pairs={{0,1},{1,2},{2,3},{3,4},{4,5},{5,6},{6,7},{7,8},{8,9},{9,10},{10,1... | collective-permute-start | bytes 147464 | tf_op jit(solution)/shard_map/while/body/eval_jaxpr/ppermute | solution.py:18
  708.2 15.7 %collective-permute-start.5 = (f32[3,8,32,128]{3,1,2,0:T(8,128)S(1)}, f32[3,8,32,128]{3,1,2,0:T(8,128)S(1)}, u32[]{:S(2)}, u32[]{:S(2)}) collective-permute-start(f32[3,8,32,128]{3,1,2,0:T(8,128)S(1)} %fusion.102), channel_id=1, source_target_pairs={{0,32},{32,64},{64,96},{96,128},{128,160},{160,192},{192,224},{1,3... | collective-permute-start | bytes 1179656 | tf_op jit(solution)/shard_map/while/body/eval_jaxpr/ppermute | solution.py:18
  (27 other events, 255.1 us)
where the time goes:
time: 729 us; the launch traced here: 725 us
  starting transfers between devices  288 us (40%)
  waiting for transfers between devices  201 us (28%)
  other arithmetic  167 us (23%)
  local copies, waits for them, and re-layouts  62.3 us (9%)
    ppermute x80, starting transfers between devices, shifted_2(): lax.ppermute(value, axis, [(source, source + steps) for source in range(f...  285 us
    ppermute x80, waiting for transfers between devices, shifted_2(): lax.ppermute(value, axis, [(source, source + steps) for source in range(f...  191 us
    add x64, other arithmetic, accumulate(): totals[1] + jnp.where(matched, curve_table[1, entry_index], 0.0)  98.1 us
    add x64, other arithmetic, accumulate(): totals[0] + jnp.where(matched, curve_table[0, entry_index], 0.0)  41.2 us
    dynamic_slice x64, local copies, waits for them, and re-layouts, accumulate(): curve_table[0, entry_index]  39.3 us
  transfers between devices with their start and end apart: 81, of which 73 were waited for; matrix products, arithmetic and copies ran while one was open for 27% of the time, Pallas kernels for 0%

commit v1 on v0

v1 whole, which is shorter than its diff:
```python
import functools

import jax
import jax.numpy as jnp
from jax import lax
from jax.experimental import pallas as pl
from jax.experimental.pallas import tpu as pltpu
from jax.sharding import PartitionSpec as P

STEPS = 2
UPDATES = 2
SWEEPS = 4
RELAX = 0.45

Z, NY, NX = 8, 32, 128
PIECE = 4
PIECES = NY // PIECE
TBL = 64
SEND, RECV = 0, 1


def next_y(v):
    return pltpu.roll(v, v.shape[-2] - 1, v.ndim - 2)


def next_x(v):
    return pltpu.roll(v, v.shape[-1] - 1, v.ndim - 1)


def prev_y(v):
    return pltpu.roll(v, 1, v.ndim - 2)


def prev_x(v):
    return pltpu.roll(v, 1, v.ndim - 1)


def curl(v, above_x, above_y):
    x, y, z = v
    return (
        (next_y(z) - z) - (above_y - y),
        (above_x - x) - (next_x(z) - z),
        (next_x(y) - y) - (next_y(x) - x),
    )


def curl_adjoint(h, below_x, below_y):
    x, y, z = h
    return (
        (below_y - y) - (prev_y(z) - z),
        (prev_x(z) - z) - (below_x - x),
        (prev_y(x) - x) - (prev_x(y) - y),
    )


def reluctance(b, base, sat):
    squared = b[0] * b[0] + b[1] * b[1] + b[2] * b[2]
    return base * (1.0 + sat * squared / (1.0 + squared))


def step_sizes(mass, nu, below, relax):
    common = mass + 2.0 * nu
    before_y, before_x = prev_y(nu), prev_x(nu)
    return (
        relax / (common + below + before_y),
        relax / (common + below + before_x),
        relax / (common + before_y + before_x),
    )


def kernel(
    T, K,
    starts, source, mass, entry, table,
    out,
    X, XC, SRC, S, E, BASE, SAT, NU, W, R, H, PQ, V9, NUM, PQS, V9S,
    PS, CB, JS, JB, PB, SYU, SYD, YL, YH, ZL, ZH, OB,
    XW, MW, BW, SW, JW, CW, RW,
    lsem, isem, psem, vsem, nsem, csem, jsem, hsem, osem,
):
    t = lax.axis_index("tm")
    k = lax.axis_index("space")
    up, down = lax.rem(k + 1, K), lax.rem(k + K - 1, K)

    def piece_of(d):
        odd = lax.rem(d, 2)
        half = d // 2
        return half * (1 - odd) + (T - 1 - half) * odd

    def group_of(i):
        low = (i < T // 2).astype(jnp.int32) if not isinstance(i, int) else int(i < T // 2)
        return 2 * i * low + (2 * T - 1 - 2 * i) * (1 - low)

    me = piece_of(t)
    right = group_of(lax.rem(me + 1, T))
    left = group_of(lax.rem(me + T - 1, T))

    def remote(src, dst, send, recv, tm, space):
        return pltpu.make_async_remote_copy(
            src_ref=src, dst_ref=dst, send_sem=send, recv_sem=recv,
            device_id=(tm, space), device_id_type=pl.DeviceIdType.MESH,
        )

    loads = [
        pltpu.make_async_copy(starts, X.at[:, 2:10], lsem.at[0]),
        pltpu.make_async_copy(source, SRC.at[:, 1:9], lsem.at[1]),
        pltpu.make_async_copy(mass, S.at[1:9], lsem.at[2]),
        pltpu.make_async_copy(entry, E.at[2:10], lsem.at[3]),
    ]
    for load in loads:
        load.start()

    barrier = pltpu.get_barrier_semaphore()

    def greet(tm, space):
        pl.semaphore_signal(
            barrier, inc=1, device_id=(tm, space), device_id_type=pl.DeviceIdType.MESH
        )

    for space in (up, down):
        for tm in (t, left, right):
            greet(tm, space)
    for r in range(1, T):
        greet(lax.rem(t + r, T), k)
    pl.semaphore_wait(barrier, 6 + T - 1)

    first = [
        remote(starts.at[:, 6:8], X.at[:, 0:2], isem.at[0, 0], isem.at[1, 0], t, up),
        remote(starts.at[:, 0:2], X.at[:, 10:12], isem.at[0, 1], isem.at[1, 1], t, down),
        remote(entry.at[6:8], E.at[0:2], isem.at[0, 2], isem.at[1, 2], t, up),
        remote(entry.at[0:1], E.at[10:11], isem.at[0, 3], isem.at[1, 3], t, down),
        remote(mass.at[7:8], S.at[0:1], isem.at[0, 4], isem.at[1, 4], t, up),
        remote(mass.at[0:1], S.at[9:10], isem.at[0, 5], isem.at[1, 5], t, down),
        remote(source.at[:, 7:8], SRC.at[:, 0:1], isem.at[0, 6], isem.at[1, 6], t, up),
        remote(source.at[:, 0:1], SRC.at[:, 9:10], isem.at[0, 7], isem.at[1, 7], t, down),
    ]
    for copy in first:
        copy.start()

    keep_bottom = jnp.where(k > 0, 1.0, 0.0).astype(jnp.float32)
    keep_top = jnp.where(k < K - 1, 1.0, 0.0).astype(jnp.float32)

    def look_up(p):
        cells = E[p]

        def body(j, acc):
            hit = cells == j
            return jnp.where(hit, table[0, j], acc[0]), jnp.where(hit, table[1, j], acc[1])

        zeros = jnp.zeros((NY, NX), jnp.float32)
        b, s = lax.fori_loop(0, TBL, body, (zeros, zeros))
        BASE[p] = b
        SAT[p] = s

    def look_up_loop(lo, hi):
        def body(p, c):
            look_up(p)
            return c

        lax.fori_loop(lo, hi, body, 0)

    loads[3].wait()
    look_up_loop(2, 10)
    for load in loads[:3]:
        load.wait()
    first[2].wait_recv()
    first[3].wait_recv()
    look_up_loop(0, 2)
    look_up(10)
    BASE[0:2] = BASE[0:2] * keep_bottom
    for c in (0, 1, 4, 5, 6, 7):
        first[c].wait_recv()
    X[:, 10:12] = X[:, 10:12] * keep_top

    for c in range(3):
        def window(p, carry, c=c):
            v = SRC[c, p]
            even, odd = pltpu.roll(v, 2, 0), pltpu.roll(v, NY - 2, 0)
            for i in range(PIECES):
                JS[i, c, p] = (odd if i % 2 else even)[8 * (i // 2):8 * (i // 2) + 8]
            return carry

        lax.fori_loop(0, 10, window, 0)

    @pl.when(t < T - 1)
    def _():
        for r in range(1, T):
            d = lax.rem(t + r, T)
            remote(JS.at[piece_of(d)], JB.at[t], jsem.at[0, r], jsem.at[1, t], d, k).start()
        pltpu.make_async_copy(JS.at[me], JB.at[t], jsem.at[1, t]).start()

    def window_of(v):
        return pltpu.roll(v, lax.rem(2 * NY + 2 - PIECE * me, NY), 0)[0:8]

    for p in range(11):
        BW[p] = window_of(BASE[p])
        SW[p] = window_of(SAT[p])
    for p in range(10):
        MW[p] = window_of(S[p]) * (1.0 / STEPS)
        RW[p] = jnp.full((8, NX), RELAX, jnp.float32) * (keep_top if p == 9 else 1.0)

    def field(ref, z):
        return [ref[c, z + 2] for c in range(3)]

    V9[0] = X[0:2, 11]
    low = field(X, -2)
    PQ[0, 0] = next_y(low[2]) - low[2] + low[1]
    PQ[0, 1] = next_x(low[2]) - low[2] + low[0]
    b = curl(low, X[0, 1], X[1, 1])
    NU[0] = reluctance(b, BASE[0], SAT[0])

    def nu_at(z, above_x, above_y):
        NU[z + 2] = reluctance(curl(field(X, z), above_x, above_y), BASE[z + 2], SAT[z + 2])

    def w_at(z, scale):
        relax = RELAX * keep_top if z == Z else RELAX
        w = step_sizes(S[z + 1] * scale, NU[z + 2], NU[z + 1], relax)
        for c in range(3):
            W[c, z + 1] = w[c]

    def intensity(ref, z, above_x, above_y):
        b = curl(field(ref, z), above_x, above_y)
        nu = NU[z + 2]
        return [nu * b[0], nu * b[1], nu * b[2]]

    def low_intensity(ref, slot):
        nu = NU[0]
        return nu * (PQ[slot, 0] - ref[1, 1]), nu * (ref[0, 1] - PQ[slot, 1])

    for z in range(-1, Z):
        nu_at(z, X[0, z + 3], X[1, z + 3])
    nu_at(Z, V9[0, 0], V9[0, 1])
    for z in range(-1, Z + 1):
        w_at(z, 1.0 / STEPS)
    hx, hy = low_intensity(X, 0)
    for z in range(-1, Z + 1):
        h = intensity(X, z, X[0, z + 3], X[1, z + 3])
        a = curl_adjoint(h, hx, hy)
        for c in range(3):
            XC[c, z + 2] = X[c, z + 2] + W[c, z + 1] * (SRC[c, z + 1] - a[c])
        hx, hy = h[0], h[1]
    h = intensity(XC, -1, XC[0, 2], XC[1, 2])
    hx, hy = h[0], h[1]
    for z in range(Z):
        h = intensity(XC, z, XC[0, z + 3], XC[1, z + 3])
        a = curl_adjoint(h, hx, hy)
        for c in range(3):
            x = XC[c, z + 2]
            drift = (1.0 / STEPS) * S[z + 1] * (X[c, z + 2] - x)
            XC[c, z + 2] = x + W[c, z + 1] * (SRC[c, z + 1] + drift - a[c])
        hx, hy = h[0], h[1]

    total = STEPS * UPDATES * SWEEPS

    def up_copy(m):
        return remote(PQS.at[m], PQ.at[m], psem.at[0, m], psem.at[1, m], t, up)

    def down_copy(m):
        return remote(V9S.at[m], V9.at[m], vsem.at[0, m], vsem.at[1, m], t, down)

    def nu_copy(u):
        return remote(NUM.at[0, u], NUM.at[1, u], nsem.at[0, u], nsem.at[1, u], t, up)

    def relax_plane(z, h, hx, hy):
        a = curl_adjoint(h, hx, hy)
        s = S[z + 1]
        new = []
        for c in range(3):
            x = X[c, z + 2]
            new.append(x + W[c, z + 1] * (R[c, z + 1] - s * x - a[c]))
            X[c, z + 2] = new[c]
        return new

    def sweep(u, i):
        m = u * SWEEPS + i
        h = intensity(X, -1, X[0, 2], X[1, 2])
        for c in range(3):
            H[c] = h[c]
        hx, hy = h[0], h[1]
        for z in range(Z):
            h = intensity(X, z, X[0, z + 3], X[1, z + 3])
            new = relax_plane(z, h, hx, hy)
            hx, hy = h[0], h[1]
            if z == 1:
                @pl.when(m < total - 1)
                def _(new=new):
                    V9S[m + 1, 0] = new[0]
                    V9S[m + 1, 1] = new[1]
                    down_copy(m + 1).start()
            if z == Z - 2:
                @pl.when(m < total - 1)
                def _(new=new):
                    PQS[m + 1, 0] = next_y(new[2]) - new[2] + new[1]
                    PQS[m + 1, 1] = next_x(new[2]) - new[2] + new[0]
                    up_copy(m + 1).start()
        H[3] = hx
        H[4] = hy

        @pl.when(m > 0)
        def _():
            down_copy(m).wait_recv()
            up_copy(m).wait_recv()

        @pl.when(i == 0)
        def _():
            @pl.when(u > 0)
            def _():
                nu_copy(u).wait_recv()
                NU[0] = NUM[1, u] * keep_bottom

            nu_at(Z, V9[m, 0], V9[m, 1])
            w_at(Z, 1.0)
            w_at(-1, 1.0)

        h = intensity(X, Z, V9[m, 0], V9[m, 1])
        relax_plane(Z, h, H[3], H[4])
        hx, hy = low_intensity(X, m)
        relax_plane(-1, [H[0], H[1], H[2]], hx, hy)

    def update(u, carry):
        @pl.when(lax.rem(u, UPDATES) == 0)
        def _():
            for p in range(10):
                for c in range(3):
                    R[c, p] = S[p] * X[c, p + 1] + SRC[c, p]

        @pl.when(u > 0)
        def _():
            nu_at(Z - 2, X[0, Z + 1], X[1, Z + 1])
            NUM[0, u] = NU[Z]
            nu_copy(u).start()

        for z in range(-1, Z):
            nu_at(z, X[0, z + 3], X[1, z + 3])
        for z in range(Z):
            w_at(z, 1.0)

        def one(i, c):
            sweep(u, i)
            return c

        lax.fori_loop(0, SWEEPS, one, 0)
        return carry

    lax.fori_loop(0, STEPS * UPDATES, update, 0)

    is_correction = jnp.where(t < T - 1, 1.0, 0.0).astype(jnp.float32)

    def pieces(z, carry):
        for c in range(3):
            v = X[c, z + 2] - is_correction * XC[c, z + 2]
            for i in range(PIECES):
                PS[i, c, z] = v[PIECE * i:PIECE * i + PIECE]
        return carry

    lax.fori_loop(0, Z, pieces, 0)
    for r in range(1, T):
        d = lax.rem(t + r, T)
        remote(PS.at[piece_of(d)], CB.at[t], csem.at[0, r], csem.at[1, t], d, k).start()
    pltpu.make_async_copy(PS.at[me], CB.at[t], csem.at[1, t]).start()

    def arrived(ref, sem):
        pltpu.make_async_copy(ref, ref, sem).wait()

    arrived(CB.at[T - 1], csem.at[1, T - 1])
    for c in range(3):
        XW[c] = jnp.zeros((Z + 4, 8, NX), jnp.float32)
        CW[c] = jnp.zeros((Z, 8, NX), jnp.float32)
    for c in range(3):
        XW[c, 2:10, 2:6] = CB[T - 1, c]

    def out_remote(n):
        return remote(PB.at[n], OB.at[me], osem.at[0, n], osem.at[1, me], n, k)

    def emit(n):
        for c in range(3):
            PB[n, c] = XW[c, 2:10, 2:6]

        @pl.when(t != n)
        def _():
            out_remote(n).start()

        @pl.when(t == n)
        def _():
            pltpu.make_async_copy(PB.at[n], OB.at[me], osem.at[1, me]).start()

    def halos(n):
        s, r = hsem.at[0, n], hsem.at[1, n]
        return [
            remote(SYU.at[n], YL.at[n, :, 2:10], s.at[0], r.at[0], right, k),
            remote(SYD.at[n], YH.at[n, :, 2:10], s.at[1], r.at[1], left, k),
            remote(PB.at[n, :, 6:8], ZL.at[n], s.at[2], r.at[2], t, up),
            remote(PB.at[n, :, 0:2], ZH.at[n], s.at[3], r.at[3], t, down),
            remote(SYU.at[n, :, 6:8], YL.at[n, :, 0:2], s.at[4], r.at[4], right, up),
            remote(SYU.at[n, :, 0:2], YL.at[n, :, 10:12], s.at[5], r.at[5], right, down),
            remote(SYD.at[n, :, 6:8], YH.at[n, :, 0:2], s.at[6], r.at[6], left, up),
            remote(SYD.at[n, :, 0:2], YH.at[n, :, 10:12], s.at[7], r.at[7], left, down),
        ]

    def propagate(n, carry):
        for c in range(3):
            SYU[n, c] = XW[c, 2:10, 4:6]
            SYD[n, c] = XW[c, 2:10, 2:4]
        emit_first = halos(n)
        emit(n)
        for copy in emit_first:
            copy.start()
        arrived(JB.at[n], jsem.at[1, n])
        arrived(CB.at[n], csem.at[1, n])
        for c in range(3):
            CW[c, :, 2:6] = CB[n, c]
        for copy in emit_first:
            copy.wait_recv()
        for c in range(3):
            XW[c, :, 0:2] = YL[n, c]
            XW[c, :, 6:8] = YH[n, c]
            XW[c, 0:2, 2:6] = ZL[n, c]
            XW[c, 10:12, 2:6] = ZH[n, c]
            XW[c, 10:12] = XW[c, 10:12] * keep_top
        x0 = [XW[c] for c in range(3)]
        b = curl([v[:-1] for v in x0], x0[0][1:], x0[1][1:])
        nu = reluctance(b, BW[...], SW[...])
        h = [nu * v for v in b]
        w = step_sizes(MW[...], nu[1:], nu[:-1], RW[...])
        a = curl_adjoint([v[1:] for v in h], h[0][:-1], h[1][:-1])
        x1 = [x0[c][1:-1] + w[c] * (JB[n, c] - a[c]) for c in range(3)]
        b = curl([v[:-1] for v in x1], x1[0][1:], x1[1][1:])
        h = [nu[1:-1] * v for v in b]
        a = curl_adjoint([v[1:] for v in h], h[0][:-1], h[1][:-1])
        for c in range(3):
            x = x1[c][1:-1]
            drift = MW[1:9] * (x0[c][2:10] - x)
            x = x + w[c][1:-1] * (JB[n, c, 1:9] + drift - a[c])
            XW[c, 2:10] = x + CW[c]
        return carry

    lax.fori_loop(0, T - 1, propagate, 0)
    emit(T - 1)

    for i in range(PIECES):
        arrived(OB.at[i], osem.at[1, i])

    def place(z, carry):
        for c in range(3):
            for i in range(PIECES):
                out[c, z, PIECE * i:PIECE * i + PIECE] = OB[i, c, z]
        return carry

    lax.fori_loop(0, Z, place, 0)

    for copy in first:
        copy.wait_send()

    def sent(m, carry):
        up_copy(m).wait_send()
        down_copy(m).wait_send()
        return carry

    lax.fori_loop(1, total, sent, 0)
    for u in range(1, STEPS * UPDATES):
        nu_copy(u).wait_send()
    for r in range(1, T):
        d = lax.rem(t + r, T)
        remote(PS.at[piece_of(d)], CB.at[t], csem.at[0, r], csem.at[1, t], d, k).wait_send()

    @pl.when(t < T - 1)
    def _():
        for r in range(1, T):
            d = lax.rem(t + r, T)
            remote(JS.at[piece_of(d)], JB.at[t], jsem.at[0, r], jsem.at[1, t], d, k).wait_send()

    def halos_sent(n, carry):
        for copy in halos(n):
            copy.wait_send()
        return carry

    lax.fori_loop(0, T - 1, halos_sent, 0)

    def out_sent(n, carry):
        @pl.when(t != n)
        def _():
            out_remote(n).wait_send()

        return carry

    lax.fori_loop(0, T, out_sent, 0)


def body(mesh, starts, source, mass_term, curve_entry, curve_table):
    T, K = mesh.shape["tm"], mesh.shape["space"]
    total = STEPS * UPDATES * SWEEPS
    f32 = jnp.float32
    vm = lambda *shape: pltpu.VMEM(shape, f32)
    dma = lambda *shape: pltpu.SemaphoreType.DMA(shape)
    scratch = [
        vm(3, Z + 4, NY, NX),
        vm(3, Z + 4, NY, NX),
        vm(3, Z + 2, NY, NX),
        vm(Z + 2, NY, NX),
        pltpu.VMEM((Z + 3, NY, NX), jnp.int32),
        vm(Z + 3, NY, NX),
        vm(Z + 3, NY, NX),
        vm(Z + 3, NY, NX),
        vm(3, Z + 2, NY, NX),
        vm(3, Z + 2, NY, NX),
        vm(5, NY, NX),
        vm(total, 2, NY, NX),
        vm(total, 2, NY, NX),
        vm(2, STEPS * UPDATES, NY, NX),
        vm(total, 2, NY, NX),
        vm(total, 2, NY, NX),
        vm(PIECES, 3, Z, PIECE, NX),
        vm(T, 3, Z, PIECE, NX),
        vm(PIECES, 3, Z + 2, 8, NX),
        vm(T, 3, Z + 2, 8, NX),
        vm(T, 3, Z, PIECE, NX),
        vm(T, 3, Z, 2, NX),
        vm(T, 3, Z, 2, NX),
        vm(T, 3, Z + 4, 2, NX),
        vm(T, 3, Z + 4, 2, NX),
        vm(T, 3, 2, PIECE, NX),
        vm(T, 3, 2, PIECE, NX),
        vm(PIECES, 3, Z, PIECE, NX),
        vm(3, Z + 4, 8, NX),
        vm(Z + 2, 8, NX),
        vm(Z + 3, 8, NX),
        vm(Z + 3, 8, NX),
        vm(Z + 2, 8, NX),
        vm(3, Z, 8, NX),
        vm(Z + 2, 8, NX),
        dma(4), dma(2, 8), dma(2, total), dma(2, total), dma(2, STEPS * UPDATES),
        dma(2, T), dma(2, T), dma(2, T, 8), dma(2, T),
    ]
    anywhere = pl.BlockSpec(memory_space=pl.ANY)
    result = pl.pallas_call(
        functools.partial(kernel, T, K),
        out_shape=jax.ShapeDtypeStruct(starts.shape[1:], f32),
        in_specs=[anywhere] * 4 + [pl.BlockSpec(memory_space=pltpu.SMEM)],
        out_specs=pl.BlockSpec(memory_space=pltpu.VMEM),
        scratch_shapes=scratch,
        compiler_params=pltpu.CompilerParams(
            collective_id=0, has_side_effects=True, vmem_limit_bytes=48 * 1024 * 1024
        ),
    )(starts[0], source[0], mass_term, curve_entry, curve_table)
    return result[None]


def solution(mesh):
    return jax.shard_map(
        functools.partial(body, mesh),
        mesh=mesh,
        in_specs=(
            P("tm", None, "space", None, None),
            P("tm", None, "space", None, None),
            P("space", None, None),
            P("space", None, None),
            P(),
        ),
        out_specs=P("tm", None, "space", None, None),
        check_vma=False,
    )
```

time: 729 us -> 107 us (0.15)
  the two profiles are of different devices: /device:TPU:106 before, /device:TPU:28 now
where the time goes in v1:
time: 107 us
  Pallas kernels  101 us (94%)
  local copies, waits for them, and re-layouts  5.22 us (5%)
    pallas_call x1, Pallas kernels, body(): pl.pallas_call(functools.partial(kernel, T, K), out_shape=jax.ShapeDtypeS...  101 us
    unnamed x11, local copies, waits for them, and re-layouts  5.22 us

profile of v1, /device:TPU:28, one launch (start us, length us, event | category | flops | bytes accessed | tf_op | source)
XLA Modules:
  0.0 106.7 jit_solution(8492773058519704372)
XLA Ops:
  0.0 0.0 copy-start.4
  0.0 0.7 copy-done.4
  0.7 0.0 copy-start
  0.7 1.0 copy-done
  1.7 0.0 copy-start.1
  1.7 1.0 copy-done.1
  2.7 0.0 copy-start.2
  2.7 0.9 copy-done.2
  3.6 0.0 copy-start.3
  3.6 0.9 copy-done.3
  4.5 101.4 %shard_map.55 = f32[3,8,32,128]{3,2,1,0:T(8,128)S(1)} custom-call(f32[3,8,32,128]{3,2,1,0:T(8,128)S(1)} %bitcast.4, f32[3,8,32,128]{3,2,1,0:T(8,128)S(1)} %bitcast.5, f32[8,32,128]{2,1,0:T(8,128)S(1)} %copy-done.2, s32[8,32,128]{2,1,0:T(8,128)S(1)} %copy-done.3, f32[2,64]{1,0:T(2,128)S(1)} %copy-done.4), custom_call_target="tpu_custom_call" | custom-call | tf_op jit(solution)/shard_map/pallas_call | solution.py:534
  105.9 0.7 copy.7
Async XLA Ops:
  0.0 0.7 copy-start.4
  0.7 1.0 copy-start
  1.7 1.0 copy-start.1
  2.7 0.9 copy-start.2
  3.6 0.9 copy-start.3

commit v2 on v1

v2 whole, which is shorter than its diff:
```python
import functools

import jax
import jax.numpy as jnp
from jax import lax
from jax.experimental import pallas as pl
from jax.experimental.pallas import tpu as pltpu
from jax.sharding import PartitionSpec as P

STEPS = 2
UPDATES = 2
SWEEPS = 4
C_SWEEPS = 2
RELAX = 0.45

Z, NY, NX = 8, 32, 128
TBL = 64
PIECE = 4
PIECES = NY // PIECE
M = 2
N = M + 1
TOP = Z + M - 1
MID = Z // 2 - 1
LAST = MID
FINE = STEPS * UPDATES * SWEEPS


def next_y(v):
    return pltpu.roll(v, v.shape[-2] - 1, v.ndim - 2)


def next_x(v):
    return pltpu.roll(v, v.shape[-1] - 1, v.ndim - 1)


def prev_y(v):
    return pltpu.roll(v, 1, v.ndim - 2)


def prev_x(v):
    return pltpu.roll(v, 1, v.ndim - 1)


def curl_xy(v, above_x, above_y):
    x, y, z = v
    return (next_y(z) - z) - (above_y - y), (above_x - x) - (next_x(z) - z)


def curl_z(v):
    return (next_x(v[1]) - v[1]) - (next_y(v[0]) - v[0])


def curl(v, above_x, above_y):
    return (*curl_xy(v, above_x, above_y), curl_z(v))


def curl_adjoint(h, below_x, below_y):
    x, y, z = h
    return (
        (below_y - y) - (prev_y(z) - z),
        (prev_x(z) - z) - (below_x - x),
        (prev_y(x) - x) - (prev_x(y) - y),
    )


def reluctance(b, base, sat):
    squared = b[0] * b[0] + b[1] * b[1] + b[2] * b[2]
    return base * (1.0 + sat * squared / (1.0 + squared))


def step_sizes(mass, nu, below, relax):
    common = mass + 2.0 * nu
    before_y, before_x = prev_y(nu), prev_x(nu)
    return (
        relax / (common + below + before_y),
        relax / (common + below + before_x),
        relax / (common + before_y + before_x),
    )


def lag(z):
    return MID - z if z <= MID else z - MID - 1


def kernel(
    T, K,
    starts, source, mass, entry, table,
    out,
    X, X0, XC, SRC, S, E, BASE, SAT, NU, NUC, W, WC, R, PQ, V9, PQS, V9S,
    OLDV, OLDH,
    PS, CB, JS, JB, PB, SYU, SYD, YL, YH, ZL, ZH, OB, XW, MW, BW, SW, CW, RW,
    lsem, isem, psem, vsem, csem, jsem, hsem, osem,
):
    t = lax.axis_index("tm")
    k = lax.axis_index("space")
    up, down = lax.rem(k + 1, K), lax.rem(k + K - 1, K)

    def piece_of(d):
        odd = lax.rem(d, 2)
        half = d // 2
        return half * (1 - odd) + (T - 1 - half) * odd

    def group_of(i):
        low = jnp.where(i < T // 2, 1, 0)
        return 2 * i * low + (2 * T - 1 - 2 * i) * (1 - low)

    me = piece_of(t)
    right = group_of(lax.rem(me + 1, T))
    left = group_of(lax.rem(me + T - 1, T))

    def remote(src, dst, send, recv, tm, space):
        return pltpu.make_async_remote_copy(
            src_ref=src, dst_ref=dst, send_sem=send, recv_sem=recv,
            device_id=(tm, space), device_id_type=pl.DeviceIdType.MESH,
        )

    loads = [
        pltpu.make_async_copy(entry, E.at[N:N + Z], lsem.at[3]),
        pltpu.make_async_copy(starts, X0.at[:, N:N + Z], lsem.at[0]),
        pltpu.make_async_copy(source, SRC.at[:, M:M + Z], lsem.at[1]),
        pltpu.make_async_copy(mass, S.at[M:M + Z], lsem.at[2]),
    ]
    for load in loads:
        load.start()

    barrier = pltpu.get_barrier_semaphore()

    def greet(tm, space):
        pl.semaphore_signal(
            barrier, inc=1, device_id=(tm, space), device_id_type=pl.DeviceIdType.MESH
        )

    for space in (up, down):
        for tm in (t, left, right):
            greet(tm, space)
    for r in range(1, T):
        greet(lax.rem(t + r, T), k)

    keep_bottom = jnp.where(k > 0, 1.0, 0.0).astype(jnp.float32)
    keep_top = jnp.where(k < K - 1, 1.0, 0.0).astype(jnp.float32)

    def look_up(lo, hi):
        def plane(p, carry):
            cells = E[p]

            def one(j, acc):
                hit = cells == j
                return jnp.where(hit, table[0, j], acc[0]), jnp.where(hit, table[1, j], acc[1])

            zeros = jnp.zeros((NY, NX), jnp.float32)
            b, s = lax.fori_loop(0, TBL, one, (zeros, zeros))
            BASE[p] = b
            SAT[p] = s
            return carry

        lax.fori_loop(lo, hi, plane, 0)

    loads[0].wait()
    look_up(N, N + Z)

    pl.semaphore_wait(barrier, 6 + T - 1)

    first = [
        remote(entry.at[Z - N:Z], E.at[0:N], isem.at[0, 2], isem.at[1, 2], t, up),
        remote(entry.at[0:M], E.at[N + Z:N + Z + M], isem.at[0, 3], isem.at[1, 3], t, down),
        remote(starts.at[:, Z - N:Z], X0.at[:, 0:N], isem.at[0, 0], isem.at[1, 0], t, up),
        remote(starts.at[:, 0:N], X0.at[:, N + Z:], isem.at[0, 1], isem.at[1, 1], t, down),
        remote(mass.at[Z - M:Z], S.at[0:M], isem.at[0, 4], isem.at[1, 4], t, up),
        remote(mass.at[0:M], S.at[M + Z:], isem.at[0, 5], isem.at[1, 5], t, down),
        remote(source.at[:, Z - M:Z], SRC.at[:, 0:M], isem.at[0, 6], isem.at[1, 6], t, up),
        remote(source.at[:, 0:M], SRC.at[:, M + Z:], isem.at[0, 7], isem.at[1, 7], t, down),
    ]
    for copy in first:
        copy.start()

    for load in loads[1:]:
        load.wait()
    for c in range(3):
        X[c, N:N + Z] = X0[c, N:N + Z]

    def scatter(pieces, there, sem, verb):
        for r in range(1, T):
            d = lax.rem(t + r, T)
            copy = remote(pieces.at[piece_of(d)], there.at[t], sem.at[0, r], sem.at[1, t], d, k)
            getattr(copy, verb)()
        if verb == "start":
            pltpu.make_async_copy(pieces.at[me], there.at[t], sem.at[1, t]).start()

    def arrived(ref, sem):
        pltpu.make_async_copy(ref, ref, sem).wait()

    def window_of(v):
        return pltpu.roll(v, lax.rem(2 * NY + 2 - PIECE * me, NY), 0)[0:8]

    def chain_windows():
        for c in range(3):
            def window(p, carry, c=c):
                v = SRC[c, p + M - 1]
                even, odd = pltpu.roll(v, 2, 0), pltpu.roll(v, NY - 2, 0)
                for i in range(PIECES):
                    JS[i, c, p] = (odd if i % 2 else even)[8 * (i // 2):8 * (i // 2) + 8]
                return carry

            lax.fori_loop(0, Z + 2, window, 0)

        @pl.when(t < T - 1)
        def _():
            scatter(JS, JB, jsem, "start")

        for p in range(Z + 3):
            BW[p] = window_of(BASE[p + M - 1])
            SW[p] = window_of(SAT[p + M - 1])
        for p in range(Z + 2):
            MW[p] = window_of(S[p + M - 1]) * (1.0 / STEPS)
            RW[p] = jnp.full((8, NX), RELAX, jnp.float32) * (keep_top if p == Z + 1 else 1.0)

    def field(ref, z):
        return [ref[c, z + N] for c in range(3)]

    def low_parts(v):
        x, y, z = v
        return next_y(z) - z + y, next_x(z) - z + x, curl_z(v)

    def old_coarse():
        def above(ref, z):
            return ref[0, z + N + 1], ref[1, z + N + 1]

        def intensity(ref, z):
            b = curl(field(ref, z), *above(ref, z))
            return [NUC[z + N] * v for v in b]

        for z in range(-2, Z + 1):
            b = curl(field(X0, z), *above(X0, z))
            NUC[z + N] = reluctance(b, BASE[z + N], SAT[z + N])
        for z in range(-1, Z + 1):
            relax = RELAX * keep_top if z >= Z else RELAX
            w = step_sizes(S[z + M] * (1.0 / STEPS), NUC[z + N], NUC[z + N - 1], relax)
            for c in range(3):
                WC[c, z + M] = w[c]
        h = intensity(X0, -2)
        hx, hy = h[0], h[1]
        for z in range(-1, Z + 1):
            h = intensity(X0, z)
            a = curl_adjoint(h, hx, hy)
            for c in range(3):
                XC[c, z + N] = X0[c, z + N] + WC[c, z + M] * (SRC[c, z + M] - a[c])
            hx, hy = h[0], h[1]
        h = intensity(XC, -1)
        hx, hy = h[0], h[1]
        for z in range(Z):
            h = intensity(XC, z)
            a = curl_adjoint(h, hx, hy)
            for c in range(3):
                x = XC[c, z + N]
                drift = (1.0 / STEPS) * S[z + M] * (X0[c, z + N] - x)
                XC[c, z + N] = x + WC[c, z + M] * (SRC[c, z + M] + drift - a[c])
            hx, hy = h[0], h[1]

    def up_copy(slot):
        return remote(PQS.at[slot], PQ.at[slot], psem.at[0, slot], psem.at[1, slot], t, up)

    def down_copy(slot):
        return remote(V9S.at[slot], V9.at[slot], vsem.at[0, slot], vsem.at[1, slot], t, down)

    def engine(sweeps, total, rhs, begin, middle):
        def plane(a, i, z):
            level = sweeps * a + i - lag(z)
            n, place = (i - lag(z)) // sweeps + a, (i - lag(z)) % sweeps
            active = jnp.logical_and(level >= 0, level < total)
            slot = jnp.clip(level, 0, total - 1)
            is_first = place == 0
            x = field(X, z)
            mass_here = S[z + M]
            if z <= MID:
                if z == -M:
                    low = PQ[slot, 0] - x[1], x[0] - PQ[slot, 1], PQ[slot, 2]
                else:
                    under = field(X, z - 1)
                    low = curl_xy(under, x[0], x[1])
                    if is_first:
                        low = (*low, curl_z(under))
                if is_first:
                    NU[z + N - 1] = reluctance(low, BASE[z + N - 1], SAT[z + N - 1])
                nu_low = NU[z + N - 1]
                hx, hy = nu_low * low[0], nu_low * low[1]
                over = (X[0, z + N + 1], X[1, z + N + 1]) if z == MID else (OLDV[0, z + M + 1], OLDV[1, z + M + 1])
                b = curl(x, *over)
                if z == MID and is_first:
                    NU[z + N] = reluctance(b, BASE[z + N], SAT[z + N])
                if z > -M:
                    OLDV[0, z + M] = x[0]
                    OLDV[1, z + M] = x[1]
            else:
                over = (V9[slot, 0], V9[slot, 1]) if z == TOP else (X[0, z + N + 1], X[1, z + N + 1])
                b = curl(x, *over)
                if is_first:
                    NU[z + N] = reluctance(b, BASE[z + N], SAT[z + N])
                hx, hy = OLDH[0, z + M - 1], OLDH[1, z + M - 1]
            nu = NU[z + N]
            h = [nu * v for v in b]
            if MID <= z < TOP:
                OLDH[0, z + M] = h[0]
                OLDH[1, z + M] = h[1]
            if is_first:
                relax = RELAX * keep_top if z >= Z else RELAX
                w = step_sizes(mass_here, nu, NU[z + N - 1], relax)
                r = rhs(n, z, mass_here, x)
                for c in range(3):
                    W[c, z + M] = w[c]
                    R[c, z + M] = r[c]
            adj = curl_adjoint(h, hx, hy)
            new = []
            for c in range(3):
                v = x[c] + W[c, z + M] * (R[c, z + M] - mass_here * x[c] - adj[c])
                v = jnp.where(active, v, x[c])
                X[c, z + N] = v
                new.append(v)

        def step(a, i):
            s = sweeps * a + i

            @pl.when(s >= LAST + 1)
            def _():
                slot = s - (LAST + M)

                @pl.when(jnp.logical_and(slot >= 1, slot < total - M))
                def _():
                    up_copy(slot).wait_recv()
                    down_copy(slot).wait_recv()

                for z in range(-M, 0):
                    plane(a, i, z)
                for z in range(TOP, Z - 1, -1):
                    plane(a, i, z)

            for z in range(MID):
                plane(a, i, z)
            for z in range(Z - 1, MID + 1, -1):
                plane(a, i, z)
            plane(a, i, MID)
            plane(a, i, MID + 1)

            slot = s + 1 - lag(M)

            @pl.when(jnp.logical_and(slot >= 1, slot < total - M))
            def _():
                V9S[slot, 0] = X[0, M + N]
                V9S[slot, 1] = X[1, M + N]
                down_copy(slot).start()
                low = low_parts(field(X, Z - 1 - M))
                for c in range(3):
                    PQS[slot, c] = low[c]
                up_copy(slot).start()

        steps = total + LAST

        def block(a, carry):
            for i in range(sweeps):
                middle(a, i)
                if i == LAST % sweeps:
                    @pl.when(a == LAST // sweeps)
                    def _():
                        begin()

                if steps % sweeps and i >= steps % sweeps:
                    @pl.when(sweeps * a + i < steps)
                    def _():
                        step(a, i)
                else:
                    step(a, i)
            return carry

        lax.fori_loop(0, (steps + sweeps - 1) // sweeps, block, 0)

    def first_message(slot):
        V9[slot] = X[0:2, N + Z + M]
        low = low_parts(field(X, -N))
        for c in range(3):
            PQ[slot, c] = low[c]

    def begin_fine():
        first[0].wait_recv()
        first[1].wait_recv()
        look_up(0, N)
        look_up(N + Z, N + Z + M)
        BASE[0:N] = BASE[0:N] * keep_bottom
        for copy in first[2:]:
            copy.wait_recv()
        for c in range(3):
            X0[c, N + Z:] = X0[c, N + Z:] * keep_top
            X[c, 0:N] = X0[c, 0:N]
            X[c, N + Z:] = X0[c, N + Z:]
        first_message(0)

    def middle_fine(a, i):
        if i == 0:
            @pl.when(jnp.logical_and(a == 2, t < T - 1))
            def _():
                old_coarse()

            @pl.when(a == 1)
            def _():
                chain_windows()

    def rhs_fine(n, z, s, x):
        fresh = lax.rem(n + UPDATES, UPDATES) == 0
        return [jnp.where(fresh, s * x[c] + SRC[c, z + M], R[c, z + M]) for c in range(3)]

    engine(
        SWEEPS, FINE, rhs_fine, begin_fine, middle_fine
    )

    def pieces(z, carry):
        for c in range(3):
            v = jnp.where(t < T - 1, X[c, z + N] - XC[c, z + N], X[c, z + N])
            for i in range(PIECES):
                PS[i, c, z] = v[PIECE * i:PIECE * i + PIECE]
        return carry

    lax.fori_loop(0, Z, pieces, 0)
    scatter(PS, CB, csem, "start")

    arrived(CB.at[T - 1], csem.at[1, T - 1])
    for c in range(3):
        XW[c] = jnp.zeros((Z + 4, 8, NX), jnp.float32)
        CW[c] = jnp.zeros((Z, 8, NX), jnp.float32)
    for c in range(3):
        XW[c, 2:10, 2:6] = CB[T - 1, c]

    def out_remote(n):
        return remote(PB.at[n], OB.at[me], osem.at[0, n], osem.at[1, me], n, k)

    def emit(n):
        for c in range(3):
            PB[n, c] = XW[c, 2:10, 2:6]

        @pl.when(t != n)
        def _():
            out_remote(n).start()

        @pl.when(t == n)
        def _():
            pltpu.make_async_copy(PB.at[n], OB.at[me], osem.at[1, me]).start()

    def halos(n):
        s, r = hsem.at[0, n], hsem.at[1, n]
        return [
            remote(SYU.at[n], YL.at[n, :, 2:10], s.at[0], r.at[0], right, k),
            remote(SYD.at[n], YH.at[n, :, 2:10], s.at[1], r.at[1], left, k),
            remote(PB.at[n, :, 6:8], ZL.at[n], s.at[2], r.at[2], t, up),
            remote(PB.at[n, :, 0:2], ZH.at[n], s.at[3], r.at[3], t, down),
            remote(SYU.at[n, :, 6:8], YL.at[n, :, 0:2], s.at[4], r.at[4], right, up),
            remote(SYU.at[n, :, 0:2], YL.at[n, :, 10:12], s.at[5], r.at[5], right, down),
            remote(SYD.at[n, :, 6:8], YH.at[n, :, 0:2], s.at[6], r.at[6], left, up),
            remote(SYD.at[n, :, 0:2], YH.at[n, :, 10:12], s.at[7], r.at[7], left, down),
        ]

    def propagate(n, carry):
        for c in range(3):
            SYU[n, c] = XW[c, 2:10, 4:6]
            SYD[n, c] = XW[c, 2:10, 2:4]
        emit_first = halos(n)
        emit(n)
        for copy in emit_first:
            copy.start()
        arrived(JB.at[n], jsem.at[1, n])
        arrived(CB.at[n], csem.at[1, n])
        for c in range(3):
            CW[c, :, 2:6] = CB[n, c]
        for copy in emit_first:
            copy.wait_recv()
        for c in range(3):
            XW[c, :, 0:2] = YL[n, c]
            XW[c, :, 6:8] = YH[n, c]
            XW[c, 0:2, 2:6] = ZL[n, c]
            XW[c, 10:12, 2:6] = ZH[n, c]
            XW[c, 10:12] = XW[c, 10:12] * keep_top
        x0 = [XW[c] for c in range(3)]
        b = curl([v[:-1] for v in x0], x0[0][1:], x0[1][1:])
        nu = reluctance(b, BW[...], SW[...])
        h = [nu * v for v in b]
        w = step_sizes(MW[...], nu[1:], nu[:-1], RW[...])
        a = curl_adjoint([v[1:] for v in h], h[0][:-1], h[1][:-1])
        x1 = [x0[c][1:-1] + w[c] * (JB[n, c] - a[c]) for c in range(3)]
        b = curl([v[:-1] for v in x1], x1[0][1:], x1[1][1:])
        h = [nu[1:-1] * v for v in b]
        a = curl_adjoint([v[1:] for v in h], h[0][:-1], h[1][:-1])
        for c in range(3):
            x = x1[c][1:-1]
            drift = MW[1:9] * (x0[c][2:10] - x)
            x = x + w[c][1:-1] * (JB[n, c, 1:9] + drift - a[c])
            XW[c, 2:10] = x + CW[c]
        return carry

    lax.fori_loop(0, T - 1, propagate, 0)
    emit(T - 1)

    for i in range(PIECES):
        arrived(OB.at[i], osem.at[1, i])

    def place(z, carry):
        for c in range(3):
            for i in range(PIECES):
                XC[c, z, PIECE * i:PIECE * i + PIECE] = OB[i, c, z]
        return carry

    lax.fori_loop(0, Z, place, 0)
    store = pltpu.make_async_copy(XC.at[:, 0:Z], out, lsem.at[0])
    store.start()

    for copy in first:
        copy.wait_send()

    def sent(m, carry):
        up_copy(m).wait_send()
        down_copy(m).wait_send()
        return carry

    lax.fori_loop(1, FINE - M, sent, 0)
    scatter(PS, CB, csem, "wait_send")

    @pl.when(t < T - 1)
    def _():
        scatter(JS, JB, jsem, "wait_send")

    def halos_sent(n, carry):
        for copy in halos(n):
            copy.wait_send()
        return carry

    lax.fori_loop(0, T - 1, halos_sent, 0)

    def out_sent(n, carry):
        @pl.when(t != n)
        def _():
            out_remote(n).wait_send()

        return carry

    lax.fori_loop(0, T, out_sent, 0)
    store.wait()


def body(mesh, starts, source, mass_term, curve_entry, curve_table):
    T, K = mesh.shape["tm"], mesh.shape["space"]
    slots = FINE
    f32 = jnp.float32
    vm = lambda *shape: pltpu.VMEM((*shape, NY, NX), f32)
    rows = lambda *shape: pltpu.VMEM(shape, f32)
    dma = lambda *shape: pltpu.SemaphoreType.DMA(shape)
    scratch = [
        vm(3, Z + 2 * N),
        vm(3, Z + 2 * N),
        vm(3, Z + 2 * N),
        vm(3, Z + 2 * M),
        vm(Z + 2 * M),
        pltpu.VMEM((Z + 2 * M + 1, NY, NX), jnp.int32),
        vm(Z + 2 * M + 1),
        vm(Z + 2 * M + 1),
        vm(Z + 2 * M + 1),
        vm(Z + 2 * M + 1),
        vm(3, Z + 2 * M),
        vm(3, Z + 2 * M),
        vm(3, Z + 2 * M),
        vm(slots, 3),
        vm(slots, 2),
        vm(slots, 3),
        vm(slots, 2),
        vm(2, Z + 2 * M),
        vm(2, Z + 2 * M),
        rows(PIECES, 3, Z, PIECE, NX),
        rows(T, 3, Z, PIECE, NX),
        rows(PIECES, 3, Z + 2, 8, NX),
        rows(T, 3, Z + 2, 8, NX),
        rows(T, 3, Z, PIECE, NX),
        rows(T, 3, Z, 2, NX),
        rows(T, 3, Z, 2, NX),
        rows(T, 3, Z + 4, 2, NX),
        rows(T, 3, Z + 4, 2, NX),
        rows(T, 3, 2, PIECE, NX),
        rows(T, 3, 2, PIECE, NX),
        rows(PIECES, 3, Z, PIECE, NX),
        rows(3, Z + 4, 8, NX),
        rows(Z + 2, 8, NX),
        rows(Z + 3, 8, NX),
        rows(Z + 3, 8, NX),
        rows(3, Z, 8, NX),
        rows(Z + 2, 8, NX),
        dma(4), dma(2, 8), dma(2, FINE), dma(2, FINE),
        dma(2, T), dma(2, T), dma(2, T, 8), dma(2, T),
    ]
    anywhere = pl.BlockSpec(memory_space=pl.ANY)
    result = pl.pallas_call(
        functools.partial(kernel, T, K),
        out_shape=jax.ShapeDtypeStruct(starts.shape[1:], f32),
        in_specs=[anywhere] * 4 + [pl.BlockSpec(memory_space=pltpu.SMEM)],
        out_specs=anywhere,
        scratch_shapes=scratch,
        compiler_params=pltpu.CompilerParams(
            collective_id=0, has_side_effects=True, vmem_limit_bytes=60 * 1024 * 1024
        ),
    )(starts[0], source[0], mass_term, curve_entry, curve_table)
    return result[None]


def solution(mesh):
    return jax.shard_map(
        functools.partial(body, mesh),
        mesh=mesh,
        in_specs=(
            P("tm", None, "space", None, None),
            P("tm", None, "space", None, None),
            P("space", None, None),
            P("space", None, None),
            P(),
        ),
        out_specs=P("tm", None, "space", None, None),
        check_vma=False,
    )
```

time: 107 us -> 92.3 us (0.86)
  Pallas kernels: 101 us -> 90.4 us
  local copies, waits for them, and re-layouts: 5.22 us -> 1.77 us
    pallas_call x1, Pallas kernels: 101 us -> 90.4 us  [body(): pl.pallas_call(functools.partial(kernel, T, K), out_shape=jax.ShapeDtypeS...]
    unnamed x11 -> x1, local copies, waits for them, and re-layouts: 5.22 us -> 1.77 us
where the time goes in v2:
time: 92.3 us; the launch traced here: 92.2 us
  Pallas kernels  90.4 us (98%)
  local copies, waits for them, and re-layouts  1.77 us (2%)
    pallas_call x1, Pallas kernels, body(): pl.pallas_call(functools.partial(kernel, T, K), out_shape=jax.ShapeDtypeS...  90.4 us

profile of v2, /device:TPU:28, one launch (start us, length us, event | category | flops | bytes accessed | tf_op | source)
XLA Modules:
  0.0 92.2 jit_solution(13519163123528936894)
XLA Ops:
  0.0 90.4 %shard_map.55 = f32[3,8,32,128]{3,2,1,0:T(8,128)} custom-call(f32[3,8,32,128]{3,2,1,0:T(8,128)} %bitcast.4, f32[3,8,32,128]{3,2,1,0:T(8,128)} %bitcast.5, f32[8,32,128]{2,1,0:T(8,128)} %mass.1, s32[8,32,128]{2,1,0:T(8,128)} %entry.1, f32[2,64]{1,0:T(2,128)} %table.1), custom_call_target="tpu_custom_call" | custom-call | tf_op jit(solution)/shard_map/pallas_call | solution.py:593
  90.4 1.8 %copy.7 = f32[1,3,8,32,128]{4,3,2,1,0:T(8,128)} copy(f32[1,3,8,32,128]{4,3,2,1,0:T(8,128)} %bitcast.3) | data formatting | bytes 786432

commit v3 on v2

--- a/solution.py
+++ b/solution.py
@@ -17,6 +17,7 @@
 TBL = 64
 PIECE = 4
 PIECES = NY // PIECE
+PACE = 1
 M = 2
 N = M + 1
 TOP = Z + M - 1
@@ -115,7 +116,7 @@
         )
 
     loads = [
-        pltpu.make_async_copy(entry, E.at[N:N + Z], lsem.at[3]),
+        pltpu.make_async_copy(entry, E, lsem.at[3]),
         pltpu.make_async_copy(starts, X0.at[:, N:N + Z], lsem.at[0]),
         pltpu.make_async_copy(source, SRC.at[:, M:M + Z], lsem.at[1]),
         pltpu.make_async_copy(mass, S.at[M:M + Z], lsem.at[2]),
@@ -141,7 +142,7 @@
 
     def look_up(lo, hi):
         def plane(p, carry):
-            cells = E[p]
+            cells = E[p - N]
 
             def one(j, acc):
                 hit = cells == j
@@ -161,8 +162,10 @@
     pl.semaphore_wait(barrier, 6 + T - 1)
 
     first = [
-        remote(entry.at[Z - N:Z], E.at[0:N], isem.at[0, 2], isem.at[1, 2], t, up),
-        remote(entry.at[0:M], E.at[N + Z:N + Z + M], isem.at[0, 3], isem.at[1, 3], t, down),
+        remote(BASE.at[Z:Z + N], BASE.at[0:N], isem.at[0, 2], isem.at[1, 2], t, up),
+        remote(BASE.at[N:N + M], BASE.at[N + Z:], isem.at[0, 3], isem.at[1, 3], t, down),
+        remote(SAT.at[Z:Z + N], SAT.at[0:N], isem.at[0, 8], isem.at[1, 8], t, up),
+        remote(SAT.at[N:N + M], SAT.at[N + Z:], isem.at[0, 9], isem.at[1, 9], t, down),
         remote(starts.at[:, Z - N:Z], X0.at[:, 0:N], isem.at[0, 0], isem.at[1, 0], t, up),
         remote(starts.at[:, 0:N], X0.at[:, N + Z:], isem.at[0, 1], isem.at[1, 1], t, down),
         remote(mass.at[Z - M:Z], S.at[0:M], isem.at[0, 4], isem.at[1, 4], t, up),
@@ -205,7 +208,7 @@
 
         @pl.when(t < T - 1)
         def _():
-            scatter(JS, JB, jsem, "start")
+            pltpu.make_async_copy(JS.at[me], JB.at[t], jsem.at[1, t]).start()
 
         for p in range(Z + 3):
             BW[p] = window_of(BASE[p + M - 1])
@@ -379,13 +382,9 @@
             PQ[slot, c] = low[c]
 
     def begin_fine():
-        first[0].wait_recv()
-        first[1].wait_recv()
-        look_up(0, N)
-        look_up(N + Z, N + Z + M)
+        for copy in first:
+            copy.wait_recv()
         BASE[0:N] = BASE[0:N] * keep_bottom
-        for copy in first[2:]:
-            copy.wait_recv()
         for c in range(3):
             X0[c, N + Z:] = X0[c, N + Z:] * keep_top
             X[c, 0:N] = X0[c, 0:N]
@@ -401,6 +400,13 @@
             @pl.when(a == 1)
             def _():
                 chain_windows()
+
+        r = (SWEEPS * a + i - SWEEPS) // PACE + 1
+
+        @pl.when(jnp.logical_and((SWEEPS * a + i) % PACE == 0, jnp.logical_and(t < T - 1, jnp.logical_and(a >= 1, r < T))))
+        def _():
+            d = lax.rem(t + r, T)
+            remote(JS.at[piece_of(d)], JB.at[t], jsem.at[0, r], jsem.at[1, t], d, k).start()
 
     def rhs_fine(n, z, s, x):
         fresh = lax.rem(n + UPDATES, UPDATES) == 0
@@ -431,9 +437,6 @@
         return remote(PB.at[n], OB.at[me], osem.at[0, n], osem.at[1, me], n, k)
 
     def emit(n):
-        for c in range(3):
-            PB[n, c] = XW[c, 2:10, 2:6]
-
         @pl.when(t != n)
         def _():
             out_remote(n).start()
@@ -460,9 +463,13 @@
             SYU[n, c] = XW[c, 2:10, 4:6]
             SYD[n, c] = XW[c, 2:10, 2:4]
         emit_first = halos(n)
+        for copy in emit_first[4:] + emit_first[:2]:
+            copy.start()
+        for c in range(3):
+            PB[n, c] = XW[c, 2:10, 2:6]
+        for copy in emit_first[2:4]:
+            copy.start()
         emit(n)
-        for copy in emit_first:
-            copy.start()
         arrived(JB.at[n], jsem.at[1, n])
         arrived(CB.at[n], csem.at[1, n])
         for c in range(3):
@@ -493,6 +500,8 @@
         return carry
 
     lax.fori_loop(0, T - 1, propagate, 0)
+    for c in range(3):
+        PB[T - 1, c] = XW[c, 2:10, 2:6]
     emit(T - 1)
 
     for i in range(PIECES):
@@ -554,7 +563,7 @@
         vm(3, Z + 2 * N),
         vm(3, Z + 2 * M),
         vm(Z + 2 * M),
-        pltpu.VMEM((Z + 2 * M + 1, NY, NX), jnp.int32),
+        pltpu.VMEM((Z, NY, NX), jnp.int32),
         vm(Z + 2 * M + 1),
         vm(Z + 2 * M + 1),
         vm(Z + 2 * M + 1),
@@ -586,7 +595,7 @@
         rows(Z + 3, 8, NX),
         rows(3, Z, 8, NX),
         rows(Z + 2, 8, NX),
-        dma(4), dma(2, 8), dma(2, FINE), dma(2, FINE),
+        dma(4), dma(2, 10), dma(2, FINE), dma(2, FINE),
         dma(2, T), dma(2, T), dma(2, T, 8), dma(2, T),
     ]
     anywhere = pl.BlockSpec(memory_space=pl.ANY)

time: 92.3 us -> 88 us (0.953)
  Pallas kernels: 90.4 us -> 86.1 us
    pallas_call x1, Pallas kernels: 90.4 us -> 86.1 us  [body(): pl.pallas_call(functools.partial(kernel, T, K), out_shape=jax.ShapeDtypeS...]
where the time goes in v3:
time: 88 us; the launch traced here: 87.9 us
  Pallas kernels  86.1 us (98%)
  local copies, waits for them, and re-layouts  1.77 us (2%)
    pallas_call x1, Pallas kernels, body(): pl.pallas_call(functools.partial(kernel, T, K), out_shape=jax.ShapeDtypeS...  86.1 us
    unnamed x1, local copies, waits for them, and re-layouts  1.77 us

profile of v3, /device:TPU:28, one launch (start us, length us, event | category | flops | bytes accessed | tf_op | source)
XLA Modules:
  0.0 87.9 jit_solution(13912543255755970620)
XLA Ops:
  0.0 86.1 %shard_map.55 = f32[3,8,32,128]{3,2,1,0:T(8,128)} custom-call(f32[3,8,32,128]{3,2,1,0:T(8,128)} %bitcast.4, f32[3,8,32,128]{3,2,1,0:T(8,128)} %bitcast.5, f32[8,32,128]{2,1,0:T(8,128)} %mass.1, s32[8,32,128]{2,1,0:T(8,128)} %entry.1, f32[2,64]{1,0:T(2,128)} %table.1), custom_call_target="tpu_custom_call" | custom-call | tf_op jit(solution)/shard_map/pallas_call | solution.py:602
  86.1 1.8 %copy.7 = f32[1,3,8,32,128]{4,3,2,1,0:T(8,128)} copy(f32[1,3,8,32,128]{4,3,2,1,0:T(8,128)} %bitcast.3) | data formatting | bytes 786432

commit v4 on v3

--- a/solution.py
+++ b/solution.py
@@ -87,10 +87,10 @@
     T, K,
     starts, source, mass, entry, table,
     out,
-    X, X0, XC, SRC, S, E, BASE, SAT, NU, NUC, W, WC, R, PQ, V9, PQS, V9S,
+    X, X0, XC, SRC, S, E, BASE, SAT, NU, NUC, W, WC, R, PQ, V9, HZ, PQS, V9S,
     OLDV, OLDH,
-    PS, CB, JS, JB, PB, SYU, SYD, YL, YH, ZL, ZH, OB, XW, MW, BW, SW, CW, RW,
-    lsem, isem, psem, vsem, csem, jsem, hsem, osem,
+    PS, CB, JS, JT, JB, JC, JW, PB, SYU, SYD, YL, YH, ZL, ZH, OB, XW, MW, BW, SW, CW, RW,
+    lsem, isem, psem, vsem, zsem, csem, jsem, ksem, hsem, osem,
 ):
     t = lax.axis_index("tm")
     k = lax.axis_index("space")
@@ -199,9 +199,11 @@
         for c in range(3):
             def window(p, carry, c=c):
                 v = SRC[c, p + M - 1]
-                even, odd = pltpu.roll(v, 2, 0), pltpu.roll(v, NY - 2, 0)
+                even, odd = pltpu.roll(v, 1, 0), pltpu.roll(v, NY - 3, 0)
                 for i in range(PIECES):
-                    JS[i, c, p] = (odd if i % 2 else even)[8 * (i // 2):8 * (i // 2) + 8]
+                    rows = (odd if i % 2 else even)[8 * (i // 2):8 * (i // 2) + 8]
+                    JS[i, c, p] = rows[0:4]
+                    JT[i, c, p] = rows[4:6]
                 return carry
 
             lax.fori_loop(0, Z + 2, window, 0)
@@ -209,6 +211,7 @@
         @pl.when(t < T - 1)
         def _():
             pltpu.make_async_copy(JS.at[me], JB.at[t], jsem.at[1, t]).start()
+            pltpu.make_async_copy(JT.at[me], JC.at[t], ksem.at[1, t]).start()
 
         for p in range(Z + 3):
             BW[p] = window_of(BASE[p + M - 1])
@@ -262,6 +265,9 @@
     def up_copy(slot):
         return remote(PQS.at[slot], PQ.at[slot], psem.at[0, slot], psem.at[1, slot], t, up)
 
+    def hz_copy(u):
+        return remote(HZ.at[0, u], HZ.at[1, u], zsem.at[0, u], zsem.at[1, u], t, up)
+
     def down_copy(slot):
         return remote(V9S.at[slot], V9.at[slot], vsem.at[0, slot], vsem.at[1, slot], t, down)
 
@@ -276,7 +282,9 @@
             mass_here = S[z + M]
             if z <= MID:
                 if z == -M:
-                    low = PQ[slot, 0] - x[1], x[0] - PQ[slot, 1], PQ[slot, 2]
+                    low = PQ[slot, 0] - x[1], x[0] - PQ[slot, 1]
+                    if is_first:
+                        low = (*low, HZ[1, jnp.clip(n, 0, total // sweeps - 1)])
                 else:
                     under = field(X, z - 1)
                     low = curl_xy(under, x[0], x[1])
@@ -330,6 +338,8 @@
                 def _():
                     up_copy(slot).wait_recv()
                     down_copy(slot).wait_recv()
+                    if (i - LAST - M) % sweeps == 0:
+                        hz_copy(a + (i - LAST - M) // sweeps).wait_recv()
 
                 for z in range(-M, 0):
                     plane(a, i, z)
@@ -351,9 +361,13 @@
                 V9S[slot, 1] = X[1, M + N]
                 down_copy(slot).start()
                 low = low_parts(field(X, Z - 1 - M))
-                for c in range(3):
-                    PQS[slot, c] = low[c]
+                PQS[slot, 0] = low[0]
+                PQS[slot, 1] = low[1]
                 up_copy(slot).start()
+                if (i + 1 - lag(M)) % sweeps == 0:
+                    u = a + (i + 1 - lag(M)) // sweeps
+                    HZ[0, u] = low[2]
+                    hz_copy(u).start()
 
         steps = total + LAST
 
@@ -378,8 +392,9 @@
     def first_message(slot):
         V9[slot] = X[0:2, N + Z + M]
         low = low_parts(field(X, -N))
-        for c in range(3):
-            PQ[slot, c] = low[c]
+        PQ[slot, 0] = low[0]
+        PQ[slot, 1] = low[1]
+        HZ[1, slot] = low[2]
 
     def begin_fine():
         for copy in first:
@@ -407,6 +422,7 @@
         def _():
             d = lax.rem(t + r, T)
             remote(JS.at[piece_of(d)], JB.at[t], jsem.at[0, r], jsem.at[1, t], d, k).start()
+            remote(JT.at[piece_of(d)], JC.at[t], ksem.at[0, r], ksem.at[1, t], d, k).start()
 
     def rhs_fine(n, z, s, x):
         fresh = lax.rem(n + UPDATES, UPDATES) == 0
@@ -427,6 +443,8 @@
     scatter(PS, CB, csem, "start")
 
     arrived(CB.at[T - 1], csem.at[1, T - 1])
+    for c in range(3):
+        JW[c] = jnp.zeros((Z + 2, 8, NX), jnp.float32)
     for c in range(3):
         XW[c] = jnp.zeros((Z + 4, 8, NX), jnp.float32)
         CW[c] = jnp.zeros((Z, 8, NX), jnp.float32)
@@ -471,6 +489,10 @@
             copy.start()
         emit(n)
         arrived(JB.at[n], jsem.at[1, n])
+        arrived(JC.at[n], ksem.at[1, n])
+        for c in range(3):
+            JW[c, :, 1:5] = JB[n, c]
+            JW[c, :, 5:7] = JC[n, c]
         arrived(CB.at[n], csem.at[1, n])
         for c in range(3):
             CW[c, :, 2:6] = CB[n, c]
@@ -488,14 +510,14 @@
         h = [nu * v for v in b]
         w = step_sizes(MW[...], nu[1:], nu[:-1], RW[...])
         a = curl_adjoint([v[1:] for v in h], h[0][:-1], h[1][:-1])
-        x1 = [x0[c][1:-1] + w[c] * (JB[n, c] - a[c]) for c in range(3)]
+        x1 = [x0[c][1:-1] + w[c] * (JW[c] - a[c]) for c in range(3)]
         b = curl([v[:-1] for v in x1], x1[0][1:], x1[1][1:])
         h = [nu[1:-1] * v for v in b]
         a = curl_adjoint([v[1:] for v in h], h[0][:-1], h[1][:-1])
         for c in range(3):
             x = x1[c][1:-1]
             drift = MW[1:9] * (x0[c][2:10] - x)
-            x = x + w[c][1:-1] * (JB[n, c, 1:9] + drift - a[c])
+            x = x + w[c][1:-1] * (JW[c, 1:9] + drift - a[c])
             XW[c, 2:10] = x + CW[c]
         return carry
 
@@ -526,11 +548,14 @@
         return carry
 
     lax.fori_loop(1, FINE - M, sent, 0)
+    for u in range(1, (FINE - M - 1) // SWEEPS + 1):
+        hz_copy(u).wait_send()
     scatter(PS, CB, csem, "wait_send")
 
     @pl.when(t < T - 1)
     def _():
         scatter(JS, JB, jsem, "wait_send")
+        scatter(JT, JC, ksem, "wait_send")
 
     def halos_sent(n, carry):
         for copy in halos(n):
@@ -571,16 +596,20 @@
         vm(3, Z + 2 * M),
         vm(3, Z + 2 * M),
         vm(3, Z + 2 * M),
-        vm(slots, 3),
         vm(slots, 2),
-        vm(slots, 3),
+        vm(slots, 2),
+        vm(2, STEPS * UPDATES),
+        vm(slots, 2),
         vm(slots, 2),
         vm(2, Z + 2 * M),
         vm(2, Z + 2 * M),
         rows(PIECES, 3, Z, PIECE, NX),
         rows(T, 3, Z, PIECE, NX),
-        rows(PIECES, 3, Z + 2, 8, NX),
-        rows(T, 3, Z + 2, 8, NX),
+        rows(PIECES, 3, Z + 2, 4, NX),
+        rows(PIECES, 3, Z + 2, 2, NX),
+        rows(T, 3, Z + 2, 4, NX),
+        rows(T, 3, Z + 2, 2, NX),
+        rows(3, Z + 2, 8, NX),
         rows(T, 3, Z, PIECE, NX),
         rows(T, 3, Z, 2, NX),
         rows(T, 3, Z, 2, NX),
@@ -595,8 +624,8 @@
         rows(Z + 3, 8, NX),
         rows(3, Z, 8, NX),
         rows(Z + 2, 8, NX),
-        dma(4), dma(2, 10), dma(2, FINE), dma(2, FINE),
-        dma(2, T), dma(2, T), dma(2, T, 8), dma(2, T),
+        dma(4), dma(2, 10), dma(2, FINE), dma(2, FINE), dma(2, STEPS * UPDATES),
+        dma(2, T), dma(2, T), dma(2, T), dma(2, T, 8), dma(2, T),
     ]
     anywhere = pl.BlockSpec(memory_space=pl.ANY)
     result = pl.pallas_call(

time: 88 us -> 83.6 us (0.950)
  Pallas kernels: 86.1 us -> 81.7 us
    pallas_call x1, Pallas kernels: 86.1 us -> 81.7 us  [body(): pl.pallas_call(functools.partial(kernel, T, K), out_shape=jax.ShapeDtypeS...]
where the time goes in v4:
time: 83.6 us; the launch traced here: 83.5 us
  Pallas kernels  81.7 us (98%)
  local copies, waits for them, and re-layouts  1.77 us (2%)
    pallas_call x1, Pallas kernels, body(): pl.pallas_call(functools.partial(kernel, T, K), out_shape=jax.ShapeDtypeS...  81.7 us
    unnamed x1, local copies, waits for them, and re-layouts  1.77 us

profile of v4, /device:TPU:28, one launch (start us, length us, event | category | flops | bytes accessed | tf_op | source)
XLA Modules:
  0.0 83.5 jit_solution(15311192517261169409)
XLA Ops:
  0.0 81.7 %shard_map.55 = f32[3,8,32,128]{3,2,1,0:T(8,128)} custom-call(f32[3,8,32,128]{3,2,1,0:T(8,128)} %bitcast.4, f32[3,8,32,128]{3,2,1,0:T(8,128)} %bitcast.5, f32[8,32,128]{2,1,0:T(8,128)} %mass.1, s32[8,32,128]{2,1,0:T(8,128)} %entry.1, f32[2,64]{1,0:T(2,128)} %table.1), custom_call_target="tpu_custom_call" | custom-call | tf_op jit(solution)/shard_map/pallas_call | solution.py:631
  81.7 1.8 %copy.7 = f32[1,3,8,32,128]{4,3,2,1,0:T(8,128)} copy(f32[1,3,8,32,128]{4,3,2,1,0:T(8,128)} %bitcast.3) | data formatting | bytes 786432

commit v5 on v4

--- a/solution.py
+++ b/solution.py
@@ -440,7 +440,12 @@
         return carry
 
     lax.fori_loop(0, Z, pieces, 0)
-    scatter(PS, CB, csem, "start")
+    urgent = jnp.logical_or(t == 0, t == T - 1)
+
+    @pl.when(urgent)
+    def _():
+        scatter(PS, CB, csem, "start")
+
 
     arrived(CB.at[T - 1], csem.at[1, T - 1])
     for c in range(3):
@@ -488,6 +493,11 @@
         for copy in emit_first[2:4]:
             copy.start()
         emit(n)
+
+        @pl.when(jnp.logical_and(n == 0, jnp.logical_not(urgent)))
+        def _():
+            scatter(PS, CB, csem, "start")
+
         arrived(JB.at[n], jsem.at[1, n])
         arrived(JC.at[n], ksem.at[1, n])
         for c in range(3):

time: 83.6 us -> 81.9 us (0.980)
  Pallas kernels: 81.7 us -> 80 us
    pallas_call x1, Pallas kernels: 81.7 us -> 80 us  [body(): pl.pallas_call(functools.partial(kernel, T, K), out_shape=jax.ShapeDtypeS...]
where the time goes in v5:
time: 81.9 us; the launch traced here: 81.7 us
  Pallas kernels  80 us (98%)
  local copies, waits for them, and re-layouts  1.77 us (2%)
    pallas_call x1, Pallas kernels, body(): pl.pallas_call(functools.partial(kernel, T, K), out_shape=jax.ShapeDtypeS...  80 us
    unnamed x1, local copies, waits for them, and re-layouts  1.77 us

profile of v5, /device:TPU:28, one launch (start us, length us, event | category | flops | bytes accessed | tf_op | source)
XLA Modules:
  0.0 81.7 jit_solution(8400932237362040760)
XLA Ops:
  0.0 80.0 %shard_map.55 = f32[3,8,32,128]{3,2,1,0:T(8,128)} custom-call(f32[3,8,32,128]{3,2,1,0:T(8,128)} %bitcast.4, f32[3,8,32,128]{3,2,1,0:T(8,128)} %bitcast.5, f32[8,32,128]{2,1,0:T(8,128)} %mass.1, s32[8,32,128]{2,1,0:T(8,128)} %entry.1, f32[2,64]{1,0:T(2,128)} %table.1), custom_call_target="tpu_custom_call" | custom-call | tf_op jit(solution)/shard_map/pallas_call | solution.py:641
  80.0 1.8 %copy.7 = f32[1,3,8,32,128]{4,3,2,1,0:T(8,128)} copy(f32[1,3,8,32,128]{4,3,2,1,0:T(8,128)} %bitcast.3) | data formatting | bytes 786432

commit v6 on v5

--- a/solution.py
+++ b/solution.py
@@ -494,7 +494,7 @@
             copy.start()
         emit(n)
 
-        @pl.when(jnp.logical_and(n == 0, jnp.logical_not(urgent)))
+        @pl.when(jnp.logical_and(n == (t >= 4).astype(jnp.int32), jnp.logical_not(urgent)))
         def _():
             scatter(PS, CB, csem, "start")
 

time: 81.9 us -> 81.6 us (level)
  no operation moved by 1% of the time
where the time goes in v6:
time: 81.6 us; the launch traced here: 81.4 us
  Pallas kernels  79.6 us (98%)
  local copies, waits for them, and re-layouts  1.77 us (2%)
    pallas_call x1, Pallas kernels, body(): pl.pallas_call(functools.partial(kernel, T, K), out_shape=jax.ShapeDtypeS...  79.6 us
    unnamed x1, local copies, waits for them, and re-layouts  1.77 us

profile of v6, /device:TPU:28, one launch (start us, length us, event | category | flops | bytes accessed | tf_op | source)
XLA Modules:
  0.0 81.4 jit_solution(5900956752283114756)
XLA Ops:
  0.0 79.6 %shard_map.55 = f32[3,8,32,128]{3,2,1,0:T(8,128)} custom-call(f32[3,8,32,128]{3,2,1,0:T(8,128)} %bitcast.4, f32[3,8,32,128]{3,2,1,0:T(8,128)} %bitcast.5, f32[8,32,128]{2,1,0:T(8,128)} %mass.1, s32[8,32,128]{2,1,0:T(8,128)} %entry.1, f32[2,64]{1,0:T(2,128)} %table.1), custom_call_target="tpu_custom_call" | custom-call | tf_op jit(solution)/shard_map/pallas_call | solution.py:641
  79.6 1.8 %copy.7 = f32[1,3,8,32,128]{4,3,2,1,0:T(8,128)} copy(f32[1,3,8,32,128]{4,3,2,1,0:T(8,128)} %bitcast.3) | data formatting | bytes 786432
